TPU v7x, 32 devices: a whole 2x2x4 slice. The times are simulated.
32 devices in a mesh: space: 8 (over z, x), mode: 4 (over y, core).
Axes of the slice: x: 2, y: 2, z: 4, core: 2. Of those that a mesh axis runs over, the one named last changes fastest.
Arguments:
- modes_in: bfloat16 [120, 16384], P('mode', 'space'), may hold values from -6 to 6
- blocks: bfloat16 [5, 576, 128, 128], P(None, 'space'), may hold values from -0.25 to 0.25
- block_cols: int32 [144, 4], P('space'), may hold values from 0 to 15
- send_slot: int32 [2048], P('space'), may hold values from 0 to 511, as said below
- recv_row: int32 [4096], P('space'), may hold values from 0 to 2048, as said below
- mix_cols: int32 [5, 120, 8], replicated, may hold values from 0 to 120, as said below
- mix_coef: float32 [5, 120, 8], replicated, as said below
Outputs:
- first_apply: bfloat16 [120, 16384], P('mode', 'space')
- second_apply: bfloat16 [120, 16384], P('mode', 'space')
Inputs may be any that keep to these rules, and one draw needn't show every extreme that they name: Interface row e of subdomain d goes to subdomain send_slot[d * 256 + e] // 64 at position send_slot[d * 256 + e] % 64. A subdomain's entries are distinct, and for each destination they fill positions from 0 upward, at most 64; one destination, the same for all subdomains, gets 64 rows from every subdomain. `recv_row`: entry o * 8 * 64 + d * 64 + p is the own degree of freedom of subdomain o at which position p from subdomain d is added; it is 2048 exactly where subdomain d sends fewer than p + 1 rows to o. Live entries may repeat. `mix_cols`: column 120 marks a padded slot. Each row of each term has from 4 to 8 live slots, both reached; live columns may repeat. `mix_coef`: zero exactly on padded slots.
All inputs are finite; a program needn't handle non-finite values.
Results may differ from a plain program's by a relative error of at most 0.022.
Values may be sent and summed in bfloat16 or wider, within the bound.
A program may use at most 64 MiB of HBM per device.

v0:
```python
import jax
import jax.numpy as jnp
from jax import lax
from jax.sharding import PartitionSpec as P


def dense_mixer(mix_cols, mix_coef):
    mode_count = mix_coef.shape[1]
    columns = jnp.arange(mode_count, dtype=jnp.int32)
    onehot_table = (mix_cols[..., None] == columns).astype(jnp.float32)
    return jnp.sum(mix_coef[..., None] * onehot_table, axis=2).astype(jnp.bfloat16)


def block_rows(field_blocks, stiffness, block_cols):
    picked = field_blocks[:, :, block_cols, :]
    return jnp.einsum("mkcnd,kcnde->mce", picked, stiffness, preferred_element_type=jnp.float32)


def local(modes_in, blocks, block_cols, send_slot, recv_row, mix_cols, mix_coef):
    chaos_mixer = dense_mixer(mix_cols, mix_coef)
    term_count = blocks.shape[0]
    block_size = blocks.shape[-1]
    out_blocks, stored = block_cols.shape
    stiffness = blocks.reshape(term_count, out_blocks, stored, block_size, block_size)
    modes_dev, owned_dofs = modes_in.shape
    owned_blocks = owned_dofs // block_size
    slot_total = recv_row.shape[0]

    def send_partials(partials):
        flat_rows = partials.reshape(modes_dev, -1)
        packed = jnp.zeros((modes_dev, slot_total), jnp.float32).at[:, send_slot].set(flat_rows)
        return lax.all_to_all(
            packed.astype(jnp.bfloat16), "space", split_axis=1, concat_axis=1, tiled=True
        ).astype(packed.dtype)

    def mix_field(field_now):
        regrouped = lax.all_to_all(field_now, "mode", split_axis=1, concat_axis=0, tiled=True)
        mixed_all = jnp.einsum(
            "kij,jn->ikn", chaos_mixer, regrouped, preferred_element_type=jnp.float32
        ).astype(jnp.bfloat16)
        return lax.all_to_all(mixed_all, "mode", split_axis=0, concat_axis=2, tiled=True)

    def one_apply(field_now):
        mixed_field = mix_field(field_now)
        field_blocks = mixed_field.reshape(modes_dev, term_count, owned_blocks, block_size)
        products = block_rows(field_blocks, stiffness, block_cols)
        arrived = send_partials(products[:, owned_blocks:])
        owned_part = products[:, :owned_blocks]
        owned_flat = owned_part.reshape(modes_dev, owned_dofs)
        summed = owned_flat.at[:, recv_row].add(arrived, mode="drop")
        return summed.astype(jnp.bfloat16)

    first_apply = one_apply(modes_in)
    second_apply = one_apply(first_apply)
    return (first_apply, second_apply)


def solution(mesh):
    in_specs = (
        P("mode", "space"),
        P(None, "space", None, None),
        P("space", None),
        P("space"),
        P("space"),
        P(),
        P(),
    )
    out_specs = (P("mode", "space"), P("mode", "space"))
    return jax.shard_map(local, mesh=mesh, in_specs=in_specs, out_specs=out_specs, check_vma=False)
```

profile of v0, /device:TPU:0, one launch (start us, length us, event | category | flops | bytes accessed | tf_op | source)
XLA Modules:
  0.0 115.5 jit_solution(5589636643510833708)
XLA Ops:
  0.6 1.0 all_to_all.62
  1.6 0.7 copy.146
  2.3 4.2 %all-to-all-start = ((bf16[30,4,512]{2,0,1:T(8,128)(2,1)}), bf16[30,4,512]{2,0,1:T(8,128)(2,1)S(1)}, u32[]{:S(2)}, u32[]{:S(2)}) async-start(bf16[30,4,512]{2,0,1:T(8,128)(2,1)} %copy.146), calls=%async_computation | async-start | bytes 262144 | tf_op jit(solution)/shard_map/all_to_all | solution.py:37
  6.5 0.9 copy.145
  7.4 0.9 copy.144
  8.3 3.5 %select_reduce_fusion = bf16[5,120,120]{2,1,0:T(8,128)(2,1)S(1)} fusion(f32[5,120,8]{2,1,0:T(8,128)S(1)} %copy.145, s32[5,120,8]{2,1,0:T(8,128)S(1)} %copy.144), kind=kLoop, calls=%fused_computation.12 | loop fusion | flops 1656000 | bytes 182400 | tf_op jit(solution)/shard_map/reduce_sum | solution.py:11
  12.2 1.2 %copy.147 = bf16[120,5,512]{2,1,0:T(8,128)(2,1)} copy(bf16[120,5,512]{2,0,1:T(8,128)(2,1)S(1)} %fusion.6) | data formatting | bytes 1228800 | tf_op jit(solution)/shard_map/convert_element_type | solution.py:40
  13.4 3.5 %all-to-all-start.1 = ((bf16[120,5,512]{2,1,0:T(8,128)(2,1)}), bf16[120,5,512]{2,1,0:T(8,128)(2,1)S(1)}, u32[]{:S(2)}, u32[]{:S(2)}) async-start(bf16[120,5,512]{2,1,0:T(8,128)(2,1)} %copy.147), calls=%async_computation.1 | async-start | bytes 1966080 | tf_op jit(solution)/shard_map/all_to_all | solution.py:41
  17.1 13.5 %all-to-all-done.1 = bf16[120,5,512]{2,1,0:T(8,128)(2,1)S(1)} async-done(((bf16[120,5,512]{2,1,0:T(8,128)(2,1)}), bf16[120,5,512]{2,1,0:T(8,128)(2,1)S(1)}, u32[]{:S(2)}, u32[]{:S(2)}) %all-to-all-start.1) | async-done | bytes 614432 | tf_op jit(solution)/shard_map/all_to_all | solution.py:41
  30.6 0.5 copy.149
  31.6 2.7 %gather_fusion = bf16[72,30,5,128]{3,1,2,0:T(8,128)(2,1)} fusion(bf16[30,5,16,128]{3,0,2,1:T(8,128)(2,1)S(1)} %copy.151, s32[1024]{0:T(1024)S(1)} %pad_clamp_fusion), kind=kCustom, calls=%fused_computation | custom fusion | bytes 5529888 | tf_op jit(solution)/shard_map/gather | solution.py:15
  34.3 2.9 %copy.152 = bf16[72,30,5,128]{3,0,2,1:T(8,128)(2,1)S(1)} copy(bf16[72,30,5,128]{3,1,2,0:T(8,128)(2,1)} %gather_fusion) | data formatting | bytes 5529600 | tf_op jit(solution)/shard_map/gather | solution.py:15
  37.2 5.4 %fusion.8 = f32[30,18,128]{2,0,1:T(8,128)S(1)} fusion(bf16[5,18,4,128,128]{4,3,2,1,0:T(8,128)(2,1)} %bitcast.79, bf16[30,5,18,4,128]{4,3,2,1,0:T(4,128)(2,1)S(1)} %bitcast.63), kind=kOutput, calls=%fused_computation.18 | convolution fusion | flops 353894400 | bytes 14837760 | tf_op jit(solution)/shard_map/mkcnd,kcnde->mce/dot_general | solution.py:16
  42.8 1.2 %scatter_custom_fusion = f32[30,512]{0,1:T(8,128)S(1)} fusion(s32[256]{0:T(256)S(1)} %compare_select_fusion.2, f32[256,30]{1,0:T(8,128)S(1)} %copy.157, f32[]{:T(128)} %constant.5.clone.1), kind=kCustom, calls=%fused_computation.22 | custom fusion | bytes 61444 | tf_op jit(solution)/shard_map/scatter | solution.py:31
  44.2 0.7 reshape.118
  45.0 6.4 %all-to-all-start.2 = ((bf16[8,2,960]{2,1,0:T(2,128)(2,1)}), bf16[8,2,960]{2,1,0:T(2,128)(2,1)S(1)}, u32[]{:S(2)}, u32[]{:S(2)}) async-start(bf16[8,2,960]{2,1,0:T(2,128)(2,1)} %reshape.118), calls=%async_computation.2 | async-start | bytes 65536 | tf_op jit(solution)/shard_map/all_to_all | solution.py:32
  51.7 6.3 %all-to-all-done.2 = bf16[8,2,960]{2,1,0:T(2,128)(2,1)S(1)} async-done(((bf16[8,2,960]{2,1,0:T(2,128)(2,1)}), bf16[8,2,960]{2,1,0:T(2,128)(2,1)S(1)}, u32[]{:S(2)}, u32[]{:S(2)}) %all-to-all-start.2) | async-done | bytes 30752 | tf_op jit(solution)/shard_map/all_to_all | solution.py:32
  58.4 3.7 %scatter_fusion = f32[30,2048]{0,1:T(8,128)S(1)} fusion(f32[30,2048]{0,1:T(8,128)S(1)} %bitcast.59, s32[512]{0:T(512)S(1)} %compare_select_fusion, f32[512,30]{1,0:T(8,128)S(1)} %copy.161), kind=kCustom, calls=%fused_computation.3 | custom fusion | flops 15360 | bytes 186368 | tf_op jit(solution)/shard_map/scatter-add | solution.py:50
  62.4 7.0 %all_to_all.86 = bf16[30,4,512]{2,0,1:T(8,128)(2,1)S(1)} all-to-all(bf16[30,4,512]{2,0,1:T(8,128)(2,1)S(1)} %copy.162), channel_id=1, replica_groups=mesh['space'=8,'mode'=4] {'mode'}, dimensions={1} | all-to-all | bytes 245760 | tf_op jit(solution)/shard_map/all_to_all | solution.py:37
  70.0 16.2 %all_to_all.87 = bf16[120,5,512]{2,1,0:T(8,128)(2,1)S(1)} all-to-all(bf16[120,5,512]{2,1,0:T(8,128)(2,1)S(1)} %copy.163), channel_id=1, replica_groups=mesh['space'=8,'mode'=4] {'mode'}, dimensions={0} | all-to-all | bytes 1228800 | tf_op jit(solution)/shard_map/all_to_all | solution.py:41
  86.2 0.5 copy.165
  87.1 2.7 %gather_fusion.1 = bf16[72,30,5,128]{3,1,2,0:T(8,128)(2,1)} fusion(bf16[30,5,16,128]{3,0,2,1:T(8,128)(2,1)S(1)} %copy.166, s32[1024]{0:T(1024)S(1)} %pad_clamp_fusion), kind=kCustom, calls=%fused_computation.1 | custom fusion | bytes 5529888 | tf_op jit(solution)/shard_map/gather | solution.py:15
  89.9 2.9 %copy.167 = bf16[72,30,5,128]{3,0,2,1:T(8,128)(2,1)S(1)} copy(bf16[72,30,5,128]{3,1,2,0:T(8,128)(2,1)} %gather_fusion.1) | data formatting | bytes 5529600 | tf_op jit(solution)/shard_map/gather | solution.py:15
  92.8 5.4 %fusion.13 = f32[30,18,128]{2,0,1:T(8,128)S(1)} fusion(bf16[5,18,4,128,128]{4,3,2,1,0:T(8,128)(2,1)} %bitcast.80, bf16[30,5,18,4,128]{4,3,2,1,0:T(4,128)(2,1)S(1)} %bitcast.64), kind=kOutput, calls=%fused_computation.19 | convolution fusion | flops 353894400 | bytes 14837760 | tf_op jit(solution)/shard_map/mkcnd,kcnde->mce/dot_general | solution.py:16
  98.4 1.2 %scatter_custom_fusion.2 = f32[30,512]{0,1:T(8,128)S(1)} fusion(s32[256]{0:T(256)S(1)} %compare_select_fusion.2, f32[256,30]{1,0:T(8,128)S(1)} %copy.172, f32[]{:T(128)} %constant.5.clone.1), kind=kCustom, calls=%fused_computation.20 | custom fusion | bytes 61444 | tf_op jit(solution)/shard_map/scatter | solution.py:31
  99.8 0.7 reshape.120
  100.5 3.3 %all-to-all-start.5 = ((bf16[8,2,960]{2,1,0:T(2,128)(2,1)}), bf16[8,2,960]{2,1,0:T(2,128)(2,1)S(1)}, u32[]{:S(2)}, u32[]{:S(2)}) async-start(bf16[8,2,960]{2,1,0:T(2,128)(2,1)} %reshape.120), calls=%async_computation.5 | async-start | bytes 65536 | tf_op jit(solution)/shard_map/all_to_all | solution.py:32
  103.9 0.9 copy.177
  104.8 0.4 copy.186
  105.1 5.3 %all-to-all-done.5 = bf16[8,2,960]{2,1,0:T(2,128)(2,1)S(1)} async-done(((bf16[8,2,960]{2,1,0:T(2,128)(2,1)}), bf16[8,2,960]{2,1,0:T(2,128)(2,1)S(1)}, u32[]{:S(2)}, u32[]{:S(2)}) %all-to-all-start.5) | async-done | bytes 30752 | tf_op jit(solution)/shard_map/all_to_all | solution.py:32
  110.9 3.7 %scatter_fusion.1 = f32[30,2048]{0,1:T(8,128)S(1)} fusion(f32[30,2048]{0,1:T(8,128)S(1)} %bitcast.58, s32[512]{0:T(512)S(1)} %compare_select_fusion, f32[512,30]{1,0:T(8,128)S(1)} %copy.176), kind=kCustom, calls=%fused_computation.5 | custom fusion | flops 15360 | bytes 186368 | tf_op jit(solution)/shard_map/scatter-add | solution.py:50
  114.6 0.9 copy.178
  (50 shorter events, 4.1 us)
Async XLA Ops:
  2.3 9.5 %all-to-all-start = ((bf16[30,4,512]{2,0,1:T(8,128)(2,1)}), bf16[30,4,512]{2,0,1:T(8,128)(2,1)S(1)}, u32[]{:S(2)}, u32[]{:S(2)}) async-start(bf16[30,4,512]{2,0,1:T(8,128)(2,1)} %copy.146), calls=%async_computation | async-start | bytes 262144 | tf_op jit(solution)/shard_map/all_to_all | solution.py:37
  7.4 9.5 %copy-start = (s32[18,4]{0,1:T(4,128)S(1)}, s32[18,4]{0,1:T(4,128)}, u32[]{:S(2)}) copy-start(s32[18,4]{0,1:T(4,128)} %param.9) | copy-start | bytes 868
  7.4 9.7 %copy-start.2 = (s32[256]{0:T(256)S(1)}, s32[256]{0:T(256)}, u32[]{:S(2)}) copy-start(s32[256]{0:T(256)} %param.10) | copy-start | bytes 3076
  13.4 17.2 %all-to-all-start.1 = ((bf16[120,5,512]{2,1,0:T(8,128)(2,1)}), bf16[120,5,512]{2,1,0:T(8,128)(2,1)S(1)}, u32[]{:S(2)}, u32[]{:S(2)}) async-start(bf16[120,5,512]{2,1,0:T(8,128)(2,1)} %copy.147), calls=%async_computation.1 | async-start | bytes 1966080 | tf_op jit(solution)/shard_map/all_to_all | solution.py:41
  37.2 14.1 %copy-start.1 = (s32[512]{0:T(512)S(1)}, s32[512]{0:T(512)}, u32[]{:S(2)}) copy-start(s32[512]{0:T(512)} %param.11) | copy-start | bytes 6148
  45.0 13.0 %all-to-all-start.2 = ((bf16[8,2,960]{2,1,0:T(2,128)(2,1)}), bf16[8,2,960]{2,1,0:T(2,128)(2,1)S(1)}, u32[]{:S(2)}, u32[]{:S(2)}) async-start(bf16[8,2,960]{2,1,0:T(2,128)(2,1)} %reshape.118), calls=%async_computation.2 | async-start | bytes 65536 | tf_op jit(solution)/shard_map/all_to_all | solution.py:32
  100.5 10.0 %all-to-all-start.5 = ((bf16[8,2,960]{2,1,0:T(2,128)(2,1)}), bf16[8,2,960]{2,1,0:T(2,128)(2,1)S(1)}, u32[]{:S(2)}, u32[]{:S(2)}) async-start(bf16[8,2,960]{2,1,0:T(2,128)(2,1)} %reshape.120), calls=%async_computation.5 | async-start | bytes 65536 | tf_op jit(solution)/shard_map/all_to_all | solution.py:32
where the time goes:
time: 116 us
  local copies, waits for them, and re-layouts  26.3 us (23%)
  waiting for transfers between devices  25.1 us (22%)
  blocking collectives  23.2 us (20%)
  starting transfers between devices  17.4 us (15%)
  matrix products  11.4 us (10%)
  other arithmetic  11.1 us (10%)
    all_to_all x1, blocking collectives, mix_field(): lax.all_to_all(mixed_all, 'mode', split_axis=0, concat_axis=2, tiled=True)  16.2 us
    all_to_all x1, waiting for transfers between devices, mix_field(): lax.all_to_all(mixed_all, 'mode', split_axis=0, concat_axis=2, tiled=True)  13.5 us
    all_to_all x2, waiting for transfers between devices, send_partials(): lax.all_to_all(packed.astype(jnp.bfloat16), 'space', split_axis=1, concat...  11.6 us
    gather x4, local copies, waits for them, and re-layouts, block_rows(): picked = field_blocks[:, :, block_cols, :]  11.3 us
    dot_general x2, matrix products, block_rows(): jnp.einsum('mkcnd,kcnde->mce', picked, stiffness, preferred_element_type=...  10.8 us
    all_to_all x2, starting transfers between devices, send_partials(): lax.all_to_all(packed.astype(jnp.bfloat16), 'space', split_axis=1, concat...  9.7 us
    scatter-add x2, other arithmetic, one_apply(): summed = owned_flat.at[:, recv_row].add(arrived, mode='drop')  7.38 us
    all_to_all x1, blocking collectives, mix_field(): lax.all_to_all(field_now, 'mode', split_axis=1, concat_axis=0, tiled=True)  7.01 us
  transfers between devices with their start and end apart: 4, of which 3 were waited for; matrix products, arithmetic and copies ran while one was open for 6% of the time, Pallas kernels for 0%

commit v1 on v0

v1 whole, which is shorter than its diff:
```python
import functools

import jax
import jax.numpy as jnp
from jax import lax
from jax.experimental import pallas as pl
from jax.experimental.pallas import tpu as pltpu
from jax.sharding import PartitionSpec as P

MESH = pl.DeviceIdType.MESH
LANES = 128
MODE_GROUPS = 4
NT = (((1,), (1,)), ((), ()))


def kernel(
    n_space,
    modes_ref,
    blocks_hbm,
    cols_ref,
    send_ref,
    recv_ref,
    mix_cols_ref,
    mix_coef_ref,
    first_ref,
    second_ref,
    stiff,
    field,
    mixed,
    mixer_f32,
    mixer,
    pack_map,
    add_map,
    own_sum,
    outbox,
    inbox,
    load_sem,
    gather_send,
    gather_recv,
    swap_send,
    swap_recv,
):
    term_count, _, block_size, _ = stiff.shape
    _, chunk_count, _, mode_rows, chunk_dofs = field.shape
    modes_dev, owned_dofs = modes_ref.shape
    chunk_blocks = chunk_dofs // block_size
    owned_blocks = owned_dofs // block_size
    out_blocks = owned_blocks + send_ref.shape[1] // block_size
    stored = stiff.shape[1] // out_blocks
    slot_total = recv_ref.shape[1]
    cap = slot_total // n_space
    per_group = LANES // cap

    me = lax.axis_index("space")
    group = lax.axis_index("mode")
    sibling = group + 1 - 2 * lax.rem(group, 2)
    partner = lax.rem(group + 2, MODE_GROUPS)
    diagonal = lax.rem(sibling + 2, MODE_GROUPS)
    others = [lax.rem(me + step, n_space) for step in range(1, n_space)]

    barrier = pltpu.get_barrier_semaphore()
    pl.semaphore_signal(barrier, inc=1, device_id={"mode": partner}, device_id_type=MESH)
    pl.semaphore_signal(barrier, inc=1, device_id={"mode": sibling}, device_id_type=MESH)
    for other in others:
        pl.semaphore_signal(barrier, inc=1, device_id={"space": other}, device_id_type=MESH)

    loads = []
    edges = [(owned_blocks, out_blocks)]
    edges += [(c * chunk_blocks, (c + 1) * chunk_blocks) for c in range(chunk_count)]
    for at, (low, high) in enumerate(edges):
        span = pl.ds(low * stored, (high - low) * stored)
        load = pltpu.make_async_copy(blocks_hbm.at[:, span], stiff.at[:, span], load_sem.at[at])
        load.start()
        loads.append(load)

    for c in range(chunk_count):
        field[0, c, group, 16:mode_rows, :] = jnp.zeros((mode_rows - 16, chunk_dofs), jnp.bfloat16)
        field[0, c, group, 0:modes_dev, :] = modes_ref[:, c * chunk_dofs : (c + 1) * chunk_dofs]

    pl.semaphore_wait(barrier, n_space + 1)

    def gather_copy(apply, kind, c):
        owner = partner if kind == 2 else group
        target = partner if kind == 1 else sibling
        return pltpu.make_async_remote_copy(
            src_ref=field.at[apply, c, owner],
            dst_ref=field.at[apply, c, owner],
            send_sem=gather_send.at[apply, kind, c],
            recv_sem=gather_recv.at[apply, kind, c],
            device_id={"mode": target},
            device_id_type=MESH,
        )

    for c in range(chunk_count):
        gather_copy(0, 1, c).start()
    for c in range(chunk_count):
        gather_copy(0, 0, c).start()

    lane_rows = lax.broadcasted_iota(jnp.int32, (LANES, send_ref.shape[1]), 0)
    shifted = lane_rows - lax.rem(me, per_group) * cap
    position = jnp.where((shifted >= 0) & (shifted < cap), shifted, -slot_total - 1)
    slots = send_ref[...]
    for o in range(n_space):
        hit = position + o * cap == slots
        pack_map[o * LANES : (o + 1) * LANES, :] = jnp.where(hit, 1.0, 0.0).astype(jnp.bfloat16)

    rows = recv_ref[...]
    tall = 2 * LANES
    dof_ids = lax.broadcasted_iota(jnp.int32, (tall, slot_total), 0)
    for at in range(0, owned_dofs, tall):
        hit = dof_ids + at == rows
        add_map[at : at + tall, :] = jnp.where(hit, 1.0, 0.0).astype(jnp.bfloat16)

    mixer_f32[...] = jnp.zeros_like(mixer_f32)
    column_ids = lax.broadcasted_iota(jnp.int32, (modes_dev, LANES), 1)
    for k in range(term_count):
        columns = mix_cols_ref[k, 0:modes_dev, :]
        weights = mix_coef_ref[k, 0:modes_dev, :]
        for g in range(1, MODE_GROUPS):
            mine = group == g
            columns = jnp.where(mine, mix_cols_ref[k, g * modes_dev : (g + 1) * modes_dev, :], columns)
            weights = jnp.where(mine, mix_coef_ref[k, g * modes_dev : (g + 1) * modes_dev, :], weights)
        padded = columns
        for g in range(1, MODE_GROUPS + 1):
            padded = padded + jnp.where(columns >= g * modes_dev, mode_rows - modes_dev, 0)
        total = jnp.zeros((modes_dev, LANES), jnp.float32)
        for s in range(columns.shape[1]):
            total = total + jnp.where(padded[:, s : s + 1] == column_ids, weights[:, s : s + 1], 0.0)
        mixer_f32[k * mode_rows : k * mode_rows + modes_dev, :] = total
    mixer[...] = mixer_f32[...].astype(jnp.bfloat16)

    def row_product(c):
        picked = [
            mixed[cols_ref[c * stored + s], k * mode_rows : (k + 1) * mode_rows, :]
            for k in range(term_count)
            for s in range(stored)
        ]
        weights = stiff[:, c * stored : (c + 1) * stored].reshape(-1, block_size)
        return jnp.dot(jnp.concatenate(picked, axis=1), weights, preferred_element_type=jnp.float32)

    def swap_copy(apply, target):
        return pltpu.make_async_remote_copy(
            src_ref=outbox.at[apply, target],
            dst_ref=inbox.at[apply, me],
            send_sem=swap_send.at[apply, target],
            recv_sem=swap_recv.at[apply, me],
            device_id={"space": target},
            device_id_type=MESH,
        )

    def arrival(apply, source):
        return pltpu.make_async_remote_copy(
            src_ref=outbox.at[apply, source],
            dst_ref=inbox.at[apply, source],
            send_sem=swap_send.at[apply, source],
            recv_sem=swap_recv.at[apply, source],
            device_id={"space": source},
            device_id_type=MESH,
        )

    for apply, out_ref in enumerate((first_ref, second_ref)):
        for c in range(chunk_count):
            gather_copy(apply, 1, c).wait_recv()
            gather_copy(apply, 2, c).start()
        for c in range(chunk_count):
            gather_copy(apply, 0, c).wait_recv()
            gather_copy(apply, 2, c).wait_recv()
            whole = field[apply, c].reshape(MODE_GROUPS * mode_rows, chunk_dofs)
            product = jnp.dot(mixer[...], whole, preferred_element_type=jnp.float32)
            product = product.astype(jnp.bfloat16)
            for b in range(chunk_blocks):
                mixed[c * chunk_blocks + b] = product[:, b * block_size : (b + 1) * block_size]

        if apply == 0:
            loads[0].wait()
        interface = [row_product(c).astype(jnp.bfloat16) for c in range(owned_blocks, out_blocks)]
        packed = lax.dot_general(
            jnp.concatenate(interface, axis=1), pack_map[...], NT, preferred_element_type=jnp.float32
        ).astype(jnp.bfloat16)
        for o in range(n_space):
            outbox[apply, o] = packed[:, o * LANES : (o + 1) * LANES]
        for other in others:
            swap_copy(apply, other).start()
        inbox[apply, me] = outbox[apply, me]

        for c in range(chunk_count):
            if apply == 0:
                loads[1 + c].wait()
            for b in range(c * chunk_blocks, (c + 1) * chunk_blocks):
                own_sum[:, b * block_size : (b + 1) * block_size] = row_product(b)

        for other in others:
            arrival(apply, other).wait_recv()
        pieces = []
        for first in range(0, n_space, per_group):
            piece = inbox[apply, first]
            for source in range(first + 1, first + per_group):
                piece = piece + inbox[apply, source]
            pieces.append(piece)
        arrived = jnp.concatenate(pieces, axis=1)
        for c in range(chunk_count):
            span = slice(c * chunk_dofs, (c + 1) * chunk_dofs)
            added = lax.dot_general(arrived, add_map[span, :], NT, preferred_element_type=jnp.float32)
            result = (own_sum[:, span] + added).astype(jnp.bfloat16)
            if apply == 0:
                field[1, c, group] = result
                gather_copy(1, 1, c).start()
                gather_copy(1, 0, c).start()
            out_ref[:, span] = result[0:modes_dev, :]

    for apply in range(2):
        for c in range(chunk_count):
            for kind in range(3):
                gather_copy(apply, kind, c).wait_send()
        for other in others:
            swap_copy(apply, other).wait_send()


def local(n_space, modes_in, blocks, block_cols, send_slot, recv_row, mix_cols, mix_coef):
    modes_dev, owned_dofs = modes_in.shape
    term_count, block_total, block_size, _ = blocks.shape
    mode_rows = -(-modes_dev // 16) * 16
    chunk_dofs = 4 * block_size
    chunk_count = owned_dofs // chunk_dofs
    slot_total = recv_row.shape[0]
    interface_rows = send_slot.shape[0]
    vmem = pl.BlockSpec(memory_space=pltpu.VMEM)
    out = jax.ShapeDtypeStruct((modes_dev, owned_dofs), jnp.bfloat16)
    call = pl.pallas_call(
        functools.partial(kernel, n_space),
        out_shape=(out, out),
        in_specs=[
            vmem,
            pl.BlockSpec(memory_space=pl.ANY),
            pl.BlockSpec(memory_space=pltpu.SMEM),
            vmem,
            vmem,
            vmem,
            vmem,
        ],
        out_specs=(vmem, vmem),
        scratch_shapes=[
            pltpu.VMEM(blocks.shape, jnp.bfloat16),
            pltpu.VMEM((2, chunk_count, MODE_GROUPS, mode_rows, chunk_dofs), jnp.bfloat16),
            pltpu.VMEM((owned_dofs // block_size, term_count * mode_rows, block_size), jnp.bfloat16),
            pltpu.VMEM((term_count * mode_rows, LANES), jnp.float32),
            pltpu.VMEM((term_count * mode_rows, LANES), jnp.bfloat16),
            pltpu.VMEM((n_space * LANES, interface_rows), jnp.bfloat16),
            pltpu.VMEM((owned_dofs, slot_total), jnp.bfloat16),
            pltpu.VMEM((mode_rows, owned_dofs), jnp.float32),
            pltpu.VMEM((2, n_space, mode_rows, LANES), jnp.bfloat16),
            pltpu.VMEM((2, n_space, mode_rows, LANES), jnp.bfloat16),
            pltpu.SemaphoreType.DMA((1 + chunk_count,)),
            pltpu.SemaphoreType.DMA((2, 3, chunk_count)),
            pltpu.SemaphoreType.DMA((2, 3, chunk_count)),
            pltpu.SemaphoreType.DMA((2, n_space)),
            pltpu.SemaphoreType.DMA((2, n_space)),
        ],
        compiler_params=pltpu.CompilerParams(
            collective_id=0, has_side_effects=True, vmem_limit_bytes=56 * 1024 * 1024
        ),
    )
    return call(
        modes_in,
        blocks,
        block_cols.reshape(-1),
        send_slot.reshape(1, -1),
        recv_row.reshape(1, -1),
        mix_cols,
        mix_coef,
    )


def solution(mesh):
    in_specs = (
        P("mode", "space"),
        P(None, "space", None, None),
        P("space", None),
        P("space"),
        P("space"),
        P(),
        P(),
    )
    out_specs = (P("mode", "space"), P("mode", "space"))
    body = functools.partial(local, mesh.shape["space"])
    return jax.shard_map(body, mesh=mesh, in_specs=in_specs, out_specs=out_specs, check_vma=False)
```

time: 116 us -> 38.9 us (0.34)
  Pallas kernels: 0 us -> 30.2 us
  waiting for transfers between devices: 25.1 us -> 0 us
  blocking collectives: 23.2 us -> 0 us
  local copies, waits for them, and re-layouts: 26.3 us -> 7.7 us
  starting transfers between devices: 17.4 us -> 0 us
  matrix products: 11.4 us -> 0 us
  other arithmetic: 11.1 us -> 0 us
    pallas_call x0 -> x1, Pallas kernels: none -> 30.2 us  [local(): call(modes_in, blocks, block_cols.reshape(-1), send_slot.reshape(1, -1),...]
    all_to_all x4 -> x0, waiting for transfers between devices: 25.1 us -> none  [the longest x1 13.5 us: mix_field(): lax.all_to_all(mixed_all, 'mode', split_axis=0, concat_axis=2, tiled=True)]
    all_to_all x2 -> x0, blocking collectives: 23.2 us -> none  [the longest x1 16.2 us: mix_field(): lax.all_to_all(mixed_all, 'mode', split_axis=0, concat_axis=2, tiled=True)]
    all_to_all x4 -> x0, starting transfers between devices: 17.4 us -> none  [the longest x2 9.7 us: send_partials(): lax.all_to_all(packed.astype(jnp.bfloat16), 'space', split_axis=1, concat...]
    dot_general x4 -> x0, matrix products: 11.4 us -> none  [the longest x2 10.8 us: block_rows(): jnp.einsum('mkcnd,kcnde->mce', picked, stiffness, preferred_element_type=...]
    gather x4 -> x0, local copies, waits for them, and re-layouts: 11.3 us -> none  [block_rows(): picked = field_blocks[:, :, block_cols, :]]
    scatter-add x2 -> x0, other arithmetic: 7.38 us -> none  [one_apply(): summed = owned_flat.at[:, recv_row].add(arrived, mode='drop')]
    reduce_sum x1 -> x0, other arithmetic: 3.49 us -> none  [dense_mixer(): jnp.sum(mix_coef[..., None] * onehot_table, axis=2).astype(jnp.bfloat16)]
  transfers between devices with their start and end apart: 4 -> 0, of which waited for: 3 -> 0; matrix products, arithmetic and copies ran while one was open for 6% -> 0% of each run, Pallas kernels for 0% -> 0%
where the time goes in v1:
time: 38.9 us; the launch traced here: 38.5 us
  Pallas kernels  30.2 us (78%)
  local copies, waits for them, and re-layouts  7.7 us (20%)
  between operations  0.64 us (2%)
    pallas_call x1, Pallas kernels, local(): call(modes_in, blocks, block_cols.reshape(-1), send_slot.reshape(1, -1),...  30.2 us
    unnamed x5, local copies, waits for them, and re-layouts  7.1 us

profile of v1, /device:TPU:0, one launch (start us, length us, event | category | flops | bytes accessed | tf_op | source)
XLA Modules:
  0.0 38.5 jit_solution(4732837392381702368)
XLA Ops:
  0.6 0.8 %copy.12 = s32[18,4]{1,0:T(8,128)S(1)} copy(s32[18,4]{0,1:T(4,128)} %param.9) | data formatting | bytes 576 | tf_op args[2]
  1.4 0.6 %reshape.13.cols_ref = s32[72]{0:T(128)} reshape(s32[18,4]{1,0:T(8,128)S(1)} %copy.12) | data formatting | bytes 576 | tf_op jit(solution)/shard_map/reshape | solution.py:266
  2.0 1.6 %copy.13.mix_cols_ref = s32[5,120,8]{2,1,0:T(8,128)} copy(s32[5,120,8]{1,2,0:T(8,128)} %param.12) | data formatting | bytes 38400 | tf_op args[5]
  3.6 1.6 %copy.14.mix_coef_ref = f32[5,120,8]{2,1,0:T(8,128)} copy(f32[5,120,8]{1,2,0:T(8,128)} %param.13) | data formatting | bytes 38400 | tf_op args[6]
  5.2 30.2 %shard_map.86 = (bf16[30,2048]{1,0:T(8,128)(2,1)}, bf16[30,2048]{1,0:T(8,128)(2,1)}) custom-call(bf16[30,2048]{1,0:T(8,128)(2,1)} %modes_ref.1, bf16[5,72,128,128]{3,2,1,0:T(8,128)(2,1)} %blocks_hbm.1, s32[72]{0:T(128)} %reshape.13.cols_ref, s32[1,256]{1,0:T(1,128)} %bitcast.3, s32[1,512]{1,0:T(1,128)} %bitcast.2, s32[5,120,8]{2,1,0:T(8,128)} %copy.13.mix_cols_ref, ...), custom_call_target="tpu_custom_call" | custom-call | tf_op jit(solution)/shard_map/pallas_call | solution.py:263
  35.4 1.6 %copy.17 = bf16[30,2048]{1,0:T(8,128)(2,1)} copy(bf16[30,2048]{1,0:T(8,128)(2,1)} %get-tuple-element.4) | data formatting | bytes 245760
  37.0 1.6 %copy.18 = bf16[30,2048]{1,0:T(8,128)(2,1)} copy(bf16[30,2048]{1,0:T(8,128)(2,1)} %get-tuple-element.5) | data formatting | bytes 245760

commit v2 on v1

v2 whole, which is shorter than its diff:
```python
import functools

import jax
import jax.numpy as jnp
from jax import lax
from jax.experimental import pallas as pl
from jax.experimental.pallas import tpu as pltpu
from jax.sharding import PartitionSpec as P

MESH = pl.DeviceIdType.MESH
LANES = 128
MODE_GROUPS = 4
NT = (((1,), (1,)), ((), ()))


def kernel(
    n_space,
    modes_ref,
    blocks_hbm,
    cols_ref,
    send_ref,
    recv_ref,
    mix_cols_ref,
    mix_coef_ref,
    first_ref,
    second_ref,
    stiff,
    field,
    sums,
    arrived,
    mixed,
    turned,
    mixer_f32,
    mixer,
    pack_map,
    add_map,
    own_sum,
    outbox,
    inbox,
    load_sem,
    gather_send,
    gather_recv,
    swap_send,
    swap_recv,
):
    term_count, _, block_size, _ = stiff.shape
    chunk_count, _, mode_rows, chunk_dofs = field.shape
    modes_dev, owned_dofs = modes_ref.shape
    all_rows = MODE_GROUPS * mode_rows
    chunk_blocks = chunk_dofs // block_size
    owned_blocks = owned_dofs // block_size
    stored, out_blocks = cols_ref.shape
    slot_total = recv_ref.shape[1]
    cap = slot_total // n_space
    per_group = LANES // cap

    me = lax.axis_index("space")
    group = lax.axis_index("mode")
    sibling = group + 1 - 2 * lax.rem(group, 2)
    partner = lax.rem(group + 2, MODE_GROUPS)
    diagonal = lax.rem(sibling + 2, MODE_GROUPS)
    others = [lax.rem(me + step, n_space) for step in range(1, n_space)]

    barrier = pltpu.get_barrier_semaphore()
    pl.semaphore_signal(barrier, inc=1, device_id={"mode": partner}, device_id_type=MESH)
    pl.semaphore_signal(barrier, inc=1, device_id={"mode": sibling}, device_id_type=MESH)
    for other in others:
        pl.semaphore_signal(barrier, inc=1, device_id={"space": other}, device_id_type=MESH)

    chunk_slots = chunk_blocks * stored
    spans = [pl.ds(owned_blocks * stored, (out_blocks - owned_blocks) * stored)]
    for step in range(chunk_count):
        spans.append(pl.ds(lax.rem(group + step, chunk_count) * chunk_slots, chunk_slots))
    loads = [
        pltpu.make_async_copy(blocks_hbm.at[:, span], stiff.at[:, span], load_sem.at[at])
        for at, span in enumerate(spans)
    ]
    for load in loads:
        load.start()

    for c in range(chunk_count):
        field[c, group, 16:mode_rows, :] = jnp.zeros((mode_rows - 16, chunk_dofs), jnp.bfloat16)
        field[c, group, 0:modes_dev, :] = modes_ref[:, c * chunk_dofs : (c + 1) * chunk_dofs]

    pl.semaphore_wait(barrier, n_space + 1)

    def hop(view, kind, at):
        owner = partner if kind == 2 else group
        target = partner if kind == 1 else sibling
        return pltpu.make_async_remote_copy(
            src_ref=view(owner),
            dst_ref=view(owner),
            send_sem=gather_send.at[kind, at],
            recv_sem=gather_recv.at[kind, at],
            device_id={"mode": target},
            device_id_type=MESH,
        )

    def field_hop(kind, c):
        return hop(lambda owner: field.at[c, owner], kind, c)

    def sums_hop(kind, p):
        return hop(lambda owner: sums.at[owner, p], kind, chunk_count + p)

    def arrived_hop(kind):
        return hop(lambda owner: arrived.at[owner], kind, chunk_count + chunk_blocks)

    for c in range(chunk_count):
        field_hop(1, c).start()
    for c in range(chunk_count):
        field_hop(0, c).start()

    turned[...] = jnp.zeros_like(turned)
    mixer_f32[...] = jnp.zeros_like(mixer_f32)
    modes_all = mix_cols_ref.shape[2]
    row_ids = lax.broadcasted_iota(jnp.int32, (LANES, modes_all), 0)
    for k in range(term_count):
        columns = mix_cols_ref[k]
        weights = mix_coef_ref[k]
        padded = columns
        for g in range(1, MODE_GROUPS + 1):
            padded = padded + jnp.where(columns >= g * modes_dev, mode_rows - modes_dev, 0)
        total = jnp.zeros((LANES, modes_all), jnp.float32)
        for s in range(columns.shape[0]):
            total = total + jnp.where(padded[s : s + 1, :] == row_ids, weights[s : s + 1, :], 0.0)
        turned[k, :, 0:modes_all] = total
        by_mode = turned[k].T
        for g in range(MODE_GROUPS):
            mixer_f32[k, g, 0:modes_dev, :] = by_mode[g * modes_dev : (g + 1) * modes_dev, :]
    mixer[...] = mixer_f32[...].astype(jnp.bfloat16)

    lane_rows = lax.broadcasted_iota(jnp.int32, (LANES, send_ref.shape[1]), 0)
    shifted = lane_rows - lax.rem(me, per_group) * cap
    position = jnp.where((shifted >= 0) & (shifted < cap), shifted, -slot_total - 1)
    slots = send_ref[...]
    for o in range(n_space):
        hit = position + o * cap == slots
        pack_map[o * LANES : (o + 1) * LANES, :] = jnp.where(hit, 1.0, 0.0).astype(jnp.bfloat16)

    rows = recv_ref[...]
    tall = 2 * LANES
    dof_ids = lax.broadcasted_iota(jnp.int32, (tall, slot_total), 0)
    for at in range(0, owned_dofs, tall):
        hit = dof_ids + at == rows
        add_map[at : at + tall, :] = jnp.where(hit, 1.0, 0.0).astype(jnp.bfloat16)

    def row_weights(c):
        return stiff[:, pl.ds(c * stored, stored)].reshape(-1, block_size)

    def own_modes_row(c):
        picked = [mixed[cols_ref[s, c], k, group] for k in range(term_count) for s in range(stored)]
        return jnp.dot(jnp.concatenate(picked, axis=1), row_weights(c), preferred_element_type=jnp.float32)

    def all_modes_row(c):
        picked = [
            mixed[cols_ref[s, c], k].reshape(all_rows, block_size)
            for k in range(term_count)
            for s in range(stored)
        ]
        return jnp.dot(jnp.concatenate(picked, axis=1), row_weights(c), preferred_element_type=jnp.float32)

    def swap_copy(apply, target):
        return pltpu.make_async_remote_copy(
            src_ref=outbox.at[apply, target],
            dst_ref=inbox.at[apply, me],
            send_sem=swap_send.at[apply, target],
            recv_sem=swap_recv.at[apply, me],
            device_id={"space": target},
            device_id_type=MESH,
        )

    def arrival(apply, source):
        return pltpu.make_async_remote_copy(
            src_ref=outbox.at[apply, source],
            dst_ref=inbox.at[apply, source],
            send_sem=swap_send.at[apply, source],
            recv_sem=swap_recv.at[apply, source],
            device_id={"space": source},
            device_id_type=MESH,
        )

    def send_interface(apply):
        interface = [own_modes_row(c).astype(jnp.bfloat16) for c in range(owned_blocks, out_blocks)]
        packed = lax.dot_general(
            jnp.concatenate(interface, axis=1), pack_map[...], NT, preferred_element_type=jnp.float32
        ).astype(jnp.bfloat16)
        for o in range(n_space):
            outbox[apply, o] = packed[:, o * LANES : (o + 1) * LANES]
        for other in others:
            swap_copy(apply, other).start()
        inbox[apply, me] = outbox[apply, me]

    def take_interface(apply):
        for other in others:
            arrival(apply, other).wait_recv()
        pieces = []
        for first in range(0, n_space, per_group):
            piece = inbox[apply, first]
            for source in range(first + 1, first + per_group):
                piece = piece + inbox[apply, source]
            pieces.append(piece)
        return jnp.concatenate(pieces, axis=1)

    def mix_all(c):
        field_hop(0, c).wait_recv()
        field_hop(2, c).wait_recv()
        whole = field[c].reshape(all_rows, chunk_dofs)
        for k in range(term_count):
            product = jnp.dot(
                mixer[k].reshape(all_rows, LANES), whole, preferred_element_type=jnp.float32
            ).astype(jnp.bfloat16)
            product = product.reshape(MODE_GROUPS, mode_rows, chunk_dofs)
            for b in range(chunk_blocks):
                mixed[c * chunk_blocks + b, k] = product[:, :, b * block_size : (b + 1) * block_size]

    for c in range(chunk_count):
        field_hop(1, c).wait_recv()
        field_hop(2, c).start()
        if c > 0:
            mix_all(c - 1)
    mix_all(chunk_count - 1)

    loads[0].wait()
    send_interface(0)
    loads[1].wait()
    for p in range(chunk_blocks):
        sums[group, p] = all_modes_row(group * chunk_blocks + p).astype(jnp.bfloat16)
        sums_hop(1, p).start()
        sums_hop(0, p).start()
    early = chunk_blocks // 2
    for p in range(early):
        sums_hop(1, p).wait_recv()
        sums_hop(2, p).start()
    arrived[group] = take_interface(0)
    arrived_hop(1).start()
    arrived_hop(0).start()
    for p in range(early, chunk_blocks):
        sums_hop(1, p).wait_recv()
        sums_hop(2, p).start()
    arrived_hop(1).wait_recv()
    arrived_hop(2).start()
    arrived_hop(0).wait_recv()
    arrived_hop(2).wait_recv()

    arrived_all = arrived[...].reshape(all_rows, slot_total)
    own_mixer = mixer[:, group].reshape(term_count * mode_rows, LANES)
    for kind, c in ((None, group), (1, partner), (0, sibling), (2, diagonal)):
        if kind in (0, 2):
            for p in range(chunk_blocks):
                sums_hop(kind, p).wait_recv()
        at = pl.multiple_of(c * chunk_dofs, chunk_dofs)
        added = lax.dot_general(
            arrived_all, add_map[pl.ds(at, chunk_dofs), :], NT, preferred_element_type=jnp.float32
        )
        own = jnp.concatenate([sums[c, p] for p in range(chunk_blocks)], axis=1)
        whole = (own.astype(jnp.float32) + added).astype(jnp.bfloat16)
        own_sum[...] = whole.reshape(MODE_GROUPS, mode_rows, chunk_dofs)
        first_ref[:, pl.ds(at, chunk_dofs)] = own_sum[group, 0:modes_dev, :]
        product = jnp.dot(own_mixer, whole, preferred_element_type=jnp.float32).astype(jnp.bfloat16)
        product = product.reshape(term_count, mode_rows, chunk_dofs)
        for b in range(chunk_blocks):
            mixed[c * chunk_blocks + b, :, group] = product[:, :, b * block_size : (b + 1) * block_size]

    send_interface(1)
    for load in loads[2:]:
        load.wait()
    rows_now = [own_modes_row(c) for c in range(owned_blocks)]
    last_arrived = take_interface(1)
    for c in range(chunk_count):
        span = slice(c * chunk_dofs, (c + 1) * chunk_dofs)
        added = lax.dot_general(last_arrived, add_map[span, :], NT, preferred_element_type=jnp.float32)
        own = jnp.concatenate(rows_now[c * chunk_blocks : (c + 1) * chunk_blocks], axis=1)
        second_ref[:, span] = (own + added)[0:modes_dev, :].astype(jnp.bfloat16)

    for kind in range(3):
        for c in range(chunk_count):
            field_hop(kind, c).wait_send()
        for p in range(chunk_blocks):
            sums_hop(kind, p).wait_send()
        arrived_hop(kind).wait_send()
    for apply in range(2):
        for other in others:
            swap_copy(apply, other).wait_send()


def local(n_space, modes_in, blocks, block_cols, send_slot, recv_row, mix_cols, mix_coef):
    modes_dev, owned_dofs = modes_in.shape
    term_count, block_total, block_size, _ = blocks.shape
    mode_rows = -(-modes_dev // 16) * 16
    chunk_count = MODE_GROUPS
    chunk_dofs = owned_dofs // chunk_count
    chunk_blocks = chunk_dofs // block_size
    owned_blocks = owned_dofs // block_size
    slot_total = recv_row.shape[0]
    interface_rows = send_slot.shape[0]
    vmem = pl.BlockSpec(memory_space=pltpu.VMEM)
    out = jax.ShapeDtypeStruct((modes_dev, owned_dofs), jnp.bfloat16)
    call = pl.pallas_call(
        functools.partial(kernel, n_space),
        out_shape=(out, out),
        in_specs=[
            vmem,
            pl.BlockSpec(memory_space=pl.ANY),
            pl.BlockSpec(memory_space=pltpu.SMEM),
            vmem,
            vmem,
            vmem,
            vmem,
        ],
        out_specs=(vmem, vmem),
        scratch_shapes=[
            pltpu.VMEM(blocks.shape, jnp.bfloat16),
            pltpu.VMEM((chunk_count, MODE_GROUPS, mode_rows, chunk_dofs), jnp.bfloat16),
            pltpu.VMEM((chunk_count, chunk_blocks, MODE_GROUPS * mode_rows, block_size), jnp.bfloat16),
            pltpu.VMEM((MODE_GROUPS, mode_rows, slot_total), jnp.bfloat16),
            pltpu.VMEM((owned_blocks, term_count, MODE_GROUPS, mode_rows, block_size), jnp.bfloat16),
            pltpu.VMEM((term_count, LANES, LANES), jnp.float32),
            pltpu.VMEM((term_count, MODE_GROUPS, mode_rows, LANES), jnp.float32),
            pltpu.VMEM((term_count, MODE_GROUPS, mode_rows, LANES), jnp.bfloat16),
            pltpu.VMEM((n_space * LANES, interface_rows), jnp.bfloat16),
            pltpu.VMEM((owned_dofs, slot_total), jnp.bfloat16),
            pltpu.VMEM((MODE_GROUPS, mode_rows, chunk_dofs), jnp.bfloat16),
            pltpu.VMEM((2, n_space, mode_rows, LANES), jnp.bfloat16),
            pltpu.VMEM((2, n_space, mode_rows, LANES), jnp.bfloat16),
            pltpu.SemaphoreType.DMA((1 + chunk_count,)),
            pltpu.SemaphoreType.DMA((3, chunk_count + chunk_blocks + 1)),
            pltpu.SemaphoreType.DMA((3, chunk_count + chunk_blocks + 1)),
            pltpu.SemaphoreType.DMA((2, n_space)),
            pltpu.SemaphoreType.DMA((2, n_space)),
        ],
        compiler_params=pltpu.CompilerParams(
            collective_id=0, has_side_effects=True, vmem_limit_bytes=56 * 1024 * 1024
        ),
    )
    return call(
        modes_in,
        blocks,
        block_cols.T,
        send_slot.reshape(1, -1),
        recv_row.reshape(1, -1),
        mix_cols.transpose(0, 2, 1),
        mix_coef.transpose(0, 2, 1),
    )


def solution(mesh):
    in_specs = (
        P("mode", "space"),
        P(None, "space", None, None),
        P("space", None),
        P("space"),
        P("space"),
        P(),
        P(),
    )
    out_specs = (P("mode", "space"), P("mode", "space"))
    body = functools.partial(local, mesh.shape["space"])
    return jax.shard_map(body, mesh=mesh, in_specs=in_specs, out_specs=out_specs, check_vma=False)
```

time: 38.9 us -> 33.5 us (0.86)
  local copies, waits for them, and re-layouts: 7.7 us -> 3.14 us
  Pallas kernels: 30.2 us -> 29.5 us
    unnamed x5 -> x2, local copies, waits for them, and re-layouts: 7.1 us -> 3.14 us
    pallas_call x1, Pallas kernels: 30.2 us -> 29.5 us  [local(): call(modes_in, blocks, block_cols.T, send_slot.reshape(1, -1), recv_row.r...]
    reshape x1 -> x0, local copies, waits for them, and re-layouts: 0.6 us -> none  [local(): block_cols.reshape(-1)]
where the time goes in v2:
time: 33.5 us; the launch traced here: 33.3 us
  Pallas kernels  29.5 us (88%)
  local copies, waits for them, and re-layouts  3.14 us (9%)
  between operations  0.64 us (2%)
    pallas_call x1, Pallas kernels, local(): call(modes_in, blocks, block_cols.T, send_slot.reshape(1, -1), recv_row.r...  29.5 us
    unnamed x2, local copies, waits for them, and re-layouts  3.14 us

profile of v2, /device:TPU:0, one launch (start us, length us, event | category | flops | bytes accessed | tf_op | source)
XLA Modules:
  0.0 33.3 jit_solution(13742456238677721879)
XLA Ops:
  0.6 29.5 %shard_map.86 = (bf16[30,2048]{1,0:T(8,128)(2,1)}, bf16[30,2048]{1,0:T(8,128)(2,1)}) custom-call(bf16[30,2048]{1,0:T(8,128)(2,1)} %modes_ref.1, bf16[5,72,128,128]{3,2,1,0:T(8,128)(2,1)} %blocks_hbm.1, s32[4,18]{1,0:T(4,128)} %bitcast.7, s32[1,256]{1,0:T(1,128)} %bitcast.9, s32[1,512]{1,0:T(1,128)} %bitcast.8, s32[5,8,120]{2,1,0:T(8,128)} %bitcast.5, ...), custom_call_target="tpu_custom_call" | custom-call | tf_op jit(solution)/shard_map/pallas_call | solution.py:335
  30.2 1.6 %copy.11 = bf16[30,2048]{1,0:T(8,128)(2,1)} copy(bf16[30,2048]{1,0:T(8,128)(2,1)} %get-tuple-element.4) | data formatting | bytes 245760
  31.7 1.6 %copy.12 = bf16[30,2048]{1,0:T(8,128)(2,1)} copy(bf16[30,2048]{1,0:T(8,128)(2,1)} %get-tuple-element.5) | data formatting | bytes 245760

commit v3 on v2

--- a/solution.py
+++ b/solution.py
@@ -10,7 +10,6 @@
 MESH = pl.DeviceIdType.MESH
 LANES = 128
 MODE_GROUPS = 4
-NT = (((1,), (1,)), ((), ()))
 
 
 def kernel(
@@ -129,20 +128,22 @@
             mixer_f32[k, g, 0:modes_dev, :] = by_mode[g * modes_dev : (g + 1) * modes_dev, :]
     mixer[...] = mixer_f32[...].astype(jnp.bfloat16)
 
-    lane_rows = lax.broadcasted_iota(jnp.int32, (LANES, send_ref.shape[1]), 0)
-    shifted = lane_rows - lax.rem(me, per_group) * cap
+    def as_column(row):
+        return jnp.broadcast_to(row.astype(jnp.float32), (LANES, LANES)).T.astype(jnp.int32)
+
+    lanes = lax.broadcasted_iota(jnp.int32, (LANES, LANES), 1)
+    shifted = lanes - lax.rem(me, per_group) * cap
     position = jnp.where((shifted >= 0) & (shifted < cap), shifted, -slot_total - 1)
-    slots = send_ref[...]
-    for o in range(n_space):
-        hit = position + o * cap == slots
-        pack_map[o * LANES : (o + 1) * LANES, :] = jnp.where(hit, 1.0, 0.0).astype(jnp.bfloat16)
-
-    rows = recv_ref[...]
-    tall = 2 * LANES
-    dof_ids = lax.broadcasted_iota(jnp.int32, (tall, slot_total), 0)
-    for at in range(0, owned_dofs, tall):
-        hit = dof_ids + at == rows
-        add_map[at : at + tall, :] = jnp.where(hit, 1.0, 0.0).astype(jnp.bfloat16)
+    for at in range(0, send_ref.shape[1], LANES):
+        slots = as_column(send_ref[:, at : at + LANES])
+        for o in range(n_space):
+            hit = position + o * cap == slots
+            pack_map[at : at + LANES, o * LANES : (o + 1) * LANES] = jnp.where(hit, 1.0, 0.0).astype(jnp.bfloat16)
+    for at in range(0, slot_total, LANES):
+        rows = as_column(recv_ref[:, at : at + LANES])
+        for b in range(owned_blocks):
+            hit = lanes + b * LANES == rows
+            add_map[at : at + LANES, b * LANES : (b + 1) * LANES] = jnp.where(hit, 1.0, 0.0).astype(jnp.bfloat16)
 
     def row_weights(c):
         return stiff[:, pl.ds(c * stored, stored)].reshape(-1, block_size)
@@ -181,8 +182,8 @@
 
     def send_interface(apply):
         interface = [own_modes_row(c).astype(jnp.bfloat16) for c in range(owned_blocks, out_blocks)]
-        packed = lax.dot_general(
-            jnp.concatenate(interface, axis=1), pack_map[...], NT, preferred_element_type=jnp.float32
+        packed = jnp.dot(
+            jnp.concatenate(interface, axis=1), pack_map[...], preferred_element_type=jnp.float32
         ).astype(jnp.bfloat16)
         for o in range(n_space):
             outbox[apply, o] = packed[:, o * LANES : (o + 1) * LANES]
@@ -249,8 +250,8 @@
             for p in range(chunk_blocks):
                 sums_hop(kind, p).wait_recv()
         at = pl.multiple_of(c * chunk_dofs, chunk_dofs)
-        added = lax.dot_general(
-            arrived_all, add_map[pl.ds(at, chunk_dofs), :], NT, preferred_element_type=jnp.float32
+        added = jnp.dot(
+            arrived_all, add_map[:, pl.ds(at, chunk_dofs)], preferred_element_type=jnp.float32
         )
         own = jnp.concatenate([sums[c, p] for p in range(chunk_blocks)], axis=1)
         whole = (own.astype(jnp.float32) + added).astype(jnp.bfloat16)
@@ -268,7 +269,7 @@
     last_arrived = take_interface(1)
     for c in range(chunk_count):
         span = slice(c * chunk_dofs, (c + 1) * chunk_dofs)
-        added = lax.dot_general(last_arrived, add_map[span, :], NT, preferred_element_type=jnp.float32)
+        added = jnp.dot(last_arrived, add_map[:, span], preferred_element_type=jnp.float32)
         own = jnp.concatenate(rows_now[c * chunk_blocks : (c + 1) * chunk_blocks], axis=1)
         second_ref[:, span] = (own + added)[0:modes_dev, :].astype(jnp.bfloat16)
 
@@ -281,6 +282,15 @@
     for apply in range(2):
         for other in others:
             swap_copy(apply, other).wait_send()
+
+
+def hand_over(first_in, second_in, first_out, second_out, sem):
+    first = pltpu.make_async_copy(first_in, first_out, sem.at[0])
+    second = pltpu.make_async_copy(second_in, second_out, sem.at[1])
+    first.start()
+    second.start()
+    first.wait()
+    second.wait()
 
 
 def local(n_space, modes_in, blocks, block_cols, send_slot, recv_row, mix_cols, mix_coef):
@@ -300,7 +310,7 @@
         out_shape=(out, out),
         in_specs=[
             vmem,
-            pl.BlockSpec(memory_space=pl.ANY),
+            pl.BlockSpec(memory_space=pltpu.HBM),
             pl.BlockSpec(memory_space=pltpu.SMEM),
             vmem,
             vmem,
@@ -317,8 +327,8 @@
             pltpu.VMEM((term_count, LANES, LANES), jnp.float32),
             pltpu.VMEM((term_count, MODE_GROUPS, mode_rows, LANES), jnp.float32),
             pltpu.VMEM((term_count, MODE_GROUPS, mode_rows, LANES), jnp.bfloat16),
-            pltpu.VMEM((n_space * LANES, interface_rows), jnp.bfloat16),
-            pltpu.VMEM((owned_dofs, slot_total), jnp.bfloat16),
+            pltpu.VMEM((interface_rows, n_space * LANES), jnp.bfloat16),
+            pltpu.VMEM((slot_total, owned_dofs), jnp.bfloat16),
             pltpu.VMEM((MODE_GROUPS, mode_rows, chunk_dofs), jnp.bfloat16),
             pltpu.VMEM((2, n_space, mode_rows, LANES), jnp.bfloat16),
             pltpu.VMEM((2, n_space, mode_rows, LANES), jnp.bfloat16),
@@ -329,10 +339,10 @@
             pltpu.SemaphoreType.DMA((2, n_space)),
         ],
         compiler_params=pltpu.CompilerParams(
-            collective_id=0, has_side_effects=True, vmem_limit_bytes=56 * 1024 * 1024
+            collective_id=0, has_side_effects=True, vmem_limit_bytes=53 * 1024 * 1024
         ),
     )
-    return call(
+    results = call(
         modes_in,
         blocks,
         block_cols.T,
@@ -341,6 +351,14 @@
         mix_cols.transpose(0, 2, 1),
         mix_coef.transpose(0, 2, 1),
     )
+    anywhere = pl.BlockSpec(memory_space=pl.ANY)
+    return pl.pallas_call(
+        hand_over,
+        out_shape=(out, out),
+        in_specs=[anywhere, anywhere],
+        out_specs=(anywhere, anywhere),
+        scratch_shapes=[pltpu.SemaphoreType.DMA((2,))],
+    )(*results)
 
 
 def solution(mesh):

time: 33.5 us -> 43.5 us (1.30)
  Pallas kernels: 29.5 us -> 36.9 us
  local copies, waits for them, and re-layouts: 3.14 us -> 5.69 us
    pallas_call x0 -> x1, Pallas kernels: none -> 9.06 us  [local(): pl.pallas_call(hand_over, out_shape=(out, out), in_specs=[anywhere, anywh...]
    unnamed x2 -> x16, local copies, waits for them, and re-layouts: 3.14 us -> 5.69 us
    pallas_call x1, Pallas kernels: 29.5 us -> 27.8 us  [local(): call(modes_in, blocks, block_cols.T, send_slot.reshape(1, -1), recv_row.r...]
where the time goes in v3:
time: 43.5 us; the launch traced here: 43.2 us
  Pallas kernels  36.9 us (85%)
  local copies, waits for them, and re-layouts  5.69 us (13%)
  between operations  0.66 us (2%)
    pallas_call x1, Pallas kernels, local(): call(modes_in, blocks, block_cols.T, send_slot.reshape(1, -1), recv_row.r...  27.8 us
    pallas_call x1, Pallas kernels, local(): pl.pallas_call(hand_over, out_shape=(out, out), in_specs=[anywhere, anywh...  9.06 us
    unnamed x16, local copies, waits for them, and re-layouts  5.69 us

profile of v3, /device:TPU:0, one launch (start us, length us, event | category | flops | bytes accessed | tf_op | source)
XLA Modules:
  0.0 43.2 jit_solution(17853334427022176890)
XLA Ops:
  0.6 0.0 copy-start
  0.6 0.9 %copy-done = bf16[30,2048]{1,0:T(8,128)(2,1)S(1)} copy-done((bf16[30,2048]{1,0:T(8,128)(2,1)S(1)}, bf16[30,2048]{1,0:T(8,128)(2,1)}, u32[]{:S(2)}) %copy-start) | copy-done | bytes 122904
  1.5 0.0 copy-start.3
  1.5 0.7 %copy-done.3 = s32[5,120,8]{1,2,0:T(8,128)S(1)} copy-done((s32[5,120,8]{1,2,0:T(8,128)S(1)}, s32[5,120,8]{1,2,0:T(8,128)}, u32[]{:S(2)}) %copy-start.3) | copy-done | bytes 19224
  2.3 0.0 copy-start.4
  2.3 0.7 %copy-done.4 = f32[5,120,8]{1,2,0:T(8,128)S(1)} copy-done((f32[5,120,8]{1,2,0:T(8,128)S(1)}, f32[5,120,8]{1,2,0:T(8,128)}, u32[]{:S(2)}) %copy-start.4) | copy-done | bytes 19224
  3.0 0.0 copy-start.5
  3.0 0.7 %copy-done.5 = s32[18,4]{0,1:T(4,128)S(1)} copy-done((s32[18,4]{0,1:T(4,128)S(1)}, s32[18,4]{0,1:T(4,128)}, u32[]{:S(2)}) %copy-start.5) | copy-done | bytes 312
  3.7 0.0 copy-start.6
  3.7 0.7 %copy-done.6 = s32[512]{0:T(512)S(1)} copy-done((s32[512]{0:T(512)S(1)}, s32[512]{0:T(512)}, u32[]{:S(2)}) %copy-start.6) | copy-done | bytes 2072
  4.4 0.0 copy-start.7
  4.4 0.7 %copy-done.7 = s32[256]{0:T(256)S(1)} copy-done((s32[256]{0:T(256)S(1)}, s32[256]{0:T(256)}, u32[]{:S(2)}) %copy-start.7) | copy-done | bytes 1048
  5.0 27.8 %shard_map.86 = (bf16[30,2048]{1,0:T(8,128)(2,1)S(1)}, bf16[30,2048]{1,0:T(8,128)(2,1)S(1)}) custom-call(bf16[30,2048]{1,0:T(8,128)(2,1)S(1)} %copy-done, bf16[5,72,128,128]{3,2,1,0:T(8,128)(2,1)} %blocks_hbm.1, s32[4,18]{1,0:T(4,128)S(1)} %bitcast.7, s32[1,256]{1,0:T(1,128)S(1)} %bitcast.9, s32[1,512]{1,0:T(1,128)S(1)} %bitcast.8, ...), custom_call_target="tpu_custom_call" | custom-call | tf_op jit(solution)/shard_map/pallas_call | solution.py:345
  32.9 0.0 copy-start.1
  32.9 0.6 %copy-done.1 = bf16[30,2048]{1,0:T(8,128)(2,1)} copy-done((bf16[30,2048]{1,0:T(8,128)(2,1)}, bf16[30,2048]{1,0:T(8,128)(2,1)S(1)}, u32[]{:S(2)}) %copy-start.1) | copy-done | bytes 122904
  33.5 0.0 copy-start.2
  33.5 0.7 %copy-done.2 = bf16[30,2048]{1,0:T(8,128)(2,1)} copy-done((bf16[30,2048]{1,0:T(8,128)(2,1)}, bf16[30,2048]{1,0:T(8,128)(2,1)S(1)}, u32[]{:S(2)}) %copy-start.2) | copy-done | bytes 122904
  34.2 9.1 %shard_map.87 = (bf16[30,2048]{1,0:T(8,128)(2,1)}, bf16[30,2048]{1,0:T(8,128)(2,1)}) custom-call(bf16[30,2048]{1,0:T(8,128)(2,1)} %copy-done.1, bf16[30,2048]{1,0:T(8,128)(2,1)} %copy-done.2), custom_call_target="tpu_custom_call" | custom-call | tf_op jit(solution)/shard_map/pallas_call | solution.py:355
Async XLA Ops:
  0.6 0.9 %copy-start = (bf16[30,2048]{1,0:T(8,128)(2,1)S(1)}, bf16[30,2048]{1,0:T(8,128)(2,1)}, u32[]{:S(2)}) copy-start(bf16[30,2048]{1,0:T(8,128)(2,1)} %modes_ref.1) | copy-start | bytes 368644
  1.5 0.7 %copy-start.3 = (s32[5,120,8]{1,2,0:T(8,128)S(1)}, s32[5,120,8]{1,2,0:T(8,128)}, u32[]{:S(2)}) copy-start(s32[5,120,8]{1,2,0:T(8,128)} %param.12) | copy-start | bytes 57604
  2.3 0.7 %copy-start.4 = (f32[5,120,8]{1,2,0:T(8,128)S(1)}, f32[5,120,8]{1,2,0:T(8,128)}, u32[]{:S(2)}) copy-start(f32[5,120,8]{1,2,0:T(8,128)} %param.13) | copy-start | bytes 57604
  3.0 0.7 %copy-start.5 = (s32[18,4]{0,1:T(4,128)S(1)}, s32[18,4]{0,1:T(4,128)}, u32[]{:S(2)}) copy-start(s32[18,4]{0,1:T(4,128)} %param.9) | copy-start | bytes 868
  3.7 0.7 %copy-start.6 = (s32[512]{0:T(512)S(1)}, s32[512]{0:T(512)}, u32[]{:S(2)}) copy-start(s32[512]{0:T(512)} %param.11) | copy-start | bytes 6148
  4.4 0.7 %copy-start.7 = (s32[256]{0:T(256)S(1)}, s32[256]{0:T(256)}, u32[]{:S(2)}) copy-start(s32[256]{0:T(256)} %param.10) | copy-start | bytes 3076
  32.9 0.7 %copy-start.1 = (bf16[30,2048]{1,0:T(8,128)(2,1)}, bf16[30,2048]{1,0:T(8,128)(2,1)S(1)}, u32[]{:S(2)}) copy-start(bf16[30,2048]{1,0:T(8,128)(2,1)S(1)} %get-tuple-element.4.first_in) | copy-start | bytes 368644
  33.5 0.7 %copy-start.2 = (bf16[30,2048]{1,0:T(8,128)(2,1)}, bf16[30,2048]{1,0:T(8,128)(2,1)S(1)}, u32[]{:S(2)}) copy-start(bf16[30,2048]{1,0:T(8,128)(2,1)S(1)} %get-tuple-element.5.second_in) | copy-start | bytes 368644

commit v4 on v3

--- a/solution.py
+++ b/solution.py
@@ -21,8 +21,7 @@
     recv_ref,
     mix_cols_ref,
     mix_coef_ref,
-    first_ref,
-    second_ref,
+    out_ref,
     stiff,
     field,
     sums,
@@ -148,9 +147,18 @@
     def row_weights(c):
         return stiff[:, pl.ds(c * stored, stored)].reshape(-1, block_size)
 
-    def own_modes_row(c):
-        picked = [mixed[cols_ref[s, c], k, group] for k in range(term_count) for s in range(stored)]
-        return jnp.dot(jnp.concatenate(picked, axis=1), row_weights(c), preferred_element_type=jnp.float32)
+    def own_modes_pair(c):
+        picked = [
+            jnp.concatenate(
+                [mixed[cols_ref[s, r], k, group] for k in range(term_count) for s in range(stored)], axis=1
+            )
+            for r in (c, c + 1)
+        ]
+        weights = jnp.concatenate([row_weights(c), row_weights(c + 1)], axis=1)
+        product = jnp.dot(jnp.concatenate(picked, axis=0), weights, preferred_element_type=jnp.float32)
+        return jnp.concatenate(
+            [product[:mode_rows, :block_size], product[mode_rows:, block_size:]], axis=1
+        )
 
     def all_modes_row(c):
         picked = [
@@ -181,7 +189,7 @@
         )
 
     def send_interface(apply):
-        interface = [own_modes_row(c).astype(jnp.bfloat16) for c in range(owned_blocks, out_blocks)]
+        interface = [own_modes_pair(c).astype(jnp.bfloat16) for c in range(owned_blocks, out_blocks, 2)]
         packed = jnp.dot(
             jnp.concatenate(interface, axis=1), pack_map[...], preferred_element_type=jnp.float32
         ).astype(jnp.bfloat16)
@@ -206,13 +214,12 @@
         field_hop(0, c).wait_recv()
         field_hop(2, c).wait_recv()
         whole = field[c].reshape(all_rows, chunk_dofs)
-        for k in range(term_count):
-            product = jnp.dot(
-                mixer[k].reshape(all_rows, LANES), whole, preferred_element_type=jnp.float32
-            ).astype(jnp.bfloat16)
-            product = product.reshape(MODE_GROUPS, mode_rows, chunk_dofs)
-            for b in range(chunk_blocks):
-                mixed[c * chunk_blocks + b, k] = product[:, :, b * block_size : (b + 1) * block_size]
+        product = jnp.dot(
+            mixer[...].reshape(term_count * all_rows, LANES), whole, preferred_element_type=jnp.float32
+        ).astype(jnp.bfloat16)
+        product = product.reshape(term_count, MODE_GROUPS, mode_rows, chunk_dofs)
+        for b in range(chunk_blocks):
+            mixed[c * chunk_blocks + b] = product[..., b * block_size : (b + 1) * block_size]
 
     for c in range(chunk_count):
         field_hop(1, c).wait_recv()
@@ -256,7 +263,7 @@
         own = jnp.concatenate([sums[c, p] for p in range(chunk_blocks)], axis=1)
         whole = (own.astype(jnp.float32) + added).astype(jnp.bfloat16)
         own_sum[...] = whole.reshape(MODE_GROUPS, mode_rows, chunk_dofs)
-        first_ref[:, pl.ds(at, chunk_dofs)] = own_sum[group, 0:modes_dev, :]
+        out_ref[0, :, pl.ds(at, chunk_dofs)] = own_sum[group, 0:modes_dev, :]
         product = jnp.dot(own_mixer, whole, preferred_element_type=jnp.float32).astype(jnp.bfloat16)
         product = product.reshape(term_count, mode_rows, chunk_dofs)
         for b in range(chunk_blocks):
@@ -265,13 +272,13 @@
     send_interface(1)
     for load in loads[2:]:
         load.wait()
-    rows_now = [own_modes_row(c) for c in range(owned_blocks)]
+    rows_now = [own_modes_pair(c) for c in range(0, owned_blocks, 2)]
     last_arrived = take_interface(1)
     for c in range(chunk_count):
         span = slice(c * chunk_dofs, (c + 1) * chunk_dofs)
         added = jnp.dot(last_arrived, add_map[:, span], preferred_element_type=jnp.float32)
-        own = jnp.concatenate(rows_now[c * chunk_blocks : (c + 1) * chunk_blocks], axis=1)
-        second_ref[:, span] = (own + added)[0:modes_dev, :].astype(jnp.bfloat16)
+        own = jnp.concatenate(rows_now[c * chunk_blocks // 2 : (c + 1) * chunk_blocks // 2], axis=1)
+        out_ref[1, :, span] = (own + added)[0:modes_dev, :].astype(jnp.bfloat16)
 
     for kind in range(3):
         for c in range(chunk_count):
@@ -282,15 +289,6 @@
     for apply in range(2):
         for other in others:
             swap_copy(apply, other).wait_send()
-
-
-def hand_over(first_in, second_in, first_out, second_out, sem):
-    first = pltpu.make_async_copy(first_in, first_out, sem.at[0])
-    second = pltpu.make_async_copy(second_in, second_out, sem.at[1])
-    first.start()
-    second.start()
-    first.wait()
-    second.wait()
 
 
 def local(n_space, modes_in, blocks, block_cols, send_slot, recv_row, mix_cols, mix_coef):
@@ -304,10 +302,10 @@
     slot_total = recv_row.shape[0]
     interface_rows = send_slot.shape[0]
     vmem = pl.BlockSpec(memory_space=pltpu.VMEM)
-    out = jax.ShapeDtypeStruct((modes_dev, owned_dofs), jnp.bfloat16)
+    out = jax.ShapeDtypeStruct((2, modes_dev, owned_dofs), jnp.bfloat16)
     call = pl.pallas_call(
         functools.partial(kernel, n_space),
-        out_shape=(out, out),
+        out_shape=out,
         in_specs=[
             vmem,
             pl.BlockSpec(memory_space=pltpu.HBM),
@@ -317,7 +315,7 @@
             vmem,
             vmem,
         ],
-        out_specs=(vmem, vmem),
+        out_specs=vmem,
         scratch_shapes=[
             pltpu.VMEM(blocks.shape, jnp.bfloat16),
             pltpu.VMEM((chunk_count, MODE_GROUPS, mode_rows, chunk_dofs), jnp.bfloat16),
@@ -339,7 +337,7 @@
             pltpu.SemaphoreType.DMA((2, n_space)),
         ],
         compiler_params=pltpu.CompilerParams(
-            collective_id=0, has_side_effects=True, vmem_limit_bytes=53 * 1024 * 1024
+            collective_id=0, has_side_effects=True, vmem_limit_bytes=56 * 1024 * 1024
         ),
     )
     results = call(
@@ -351,14 +349,8 @@
         mix_cols.transpose(0, 2, 1),
         mix_coef.transpose(0, 2, 1),
     )
-    anywhere = pl.BlockSpec(memory_space=pl.ANY)
-    return pl.pallas_call(
-        hand_over,
-        out_shape=(out, out),
-        in_specs=[anywhere, anywhere],
-        out_specs=(anywhere, anywhere),
-        scratch_shapes=[pltpu.SemaphoreType.DMA((2,))],
-    )(*results)
+
+    return results[0], results[1]
 
 
 def solution(mesh):

time: 43.5 us -> 31.8 us (0.73)
  Pallas kernels: 36.9 us -> 29.4 us
  local copies, waits for them, and re-layouts: 5.69 us -> 1.68 us
    pallas_call x1 -> x0, Pallas kernels: 9.06 us -> none  [local(): pl.pallas_call(hand_over, out_shape=(out, out), in_specs=[anywhere, anywh...]
    unnamed x16 -> x0, local copies, waits for them, and re-layouts: 5.69 us -> none
    squeeze x0 -> x1, local copies, waits for them, and re-layouts: none -> 1.68 us  [local(): return (results[0], results[1])]
    pallas_call x1, Pallas kernels: 27.8 us -> 29.4 us  [local(): call(modes_in, blocks, block_cols.T, send_slot.reshape(1, -1), recv_row.r...]
where the time goes in v4:
time: 31.8 us; the launch traced here: 31.7 us
  Pallas kernels  29.4 us (92%)
  local copies, waits for them, and re-layouts  1.68 us (5%)
  between operations  0.64 us (2%)
    pallas_call x1, Pallas kernels, local(): call(modes_in, blocks, block_cols.T, send_slot.reshape(1, -1), recv_row.r...  29.4 us
    squeeze x1, local copies, waits for them, and re-layouts, local(): return (results[0], results[1])  1.68 us

profile of v4, /device:TPU:0, one launch (start us, length us, event | category | flops | bytes accessed | tf_op | source)
XLA Modules:
  0.0 31.7 jit_solution(499482882323815828)
XLA Ops:
  0.6 29.4 %shard_map.86 = bf16[2,30,2048]{2,1,0:T(8,128)(2,1)} custom-call(bf16[30,2048]{1,0:T(8,128)(2,1)} %modes_ref.1, bf16[5,72,128,128]{3,2,1,0:T(8,128)(2,1)} %blocks_hbm.1, s32[4,18]{1,0:T(4,128)} %bitcast.11, s32[1,256]{1,0:T(1,128)} %bitcast.13, s32[1,512]{1,0:T(1,128)} %bitcast.12, s32[5,8,120]{2,1,0:T(8,128)} %bitcast.9, f32[5,8,120]{2,1,0:T(8,128)} %bitcast.10), custom_call_target="tpu_custom_call" | custom-call | tf_op jit(solution)/shard_map/pallas_call | solution.py:343
  30.0 1.7 %slice_bitcast_fusion = (bf16[30,2048]{1,0:T(8,128)(2,1)}, bf16[30,2048]{1,0:T(8,128)(2,1)}) fusion(bf16[2,30,2048]{2,1,0:T(8,128)(2,1)} %shard_map.86), kind=kLoop, calls=%fused_computation | loop fusion | bytes 491520 | tf_op jit(solution)/shard_map/squeeze | solution.py:353

commit v5 on v4

--- a/solution.py
+++ b/solution.py
@@ -50,13 +50,15 @@
     stored, out_blocks = cols_ref.shape
     slot_total = recv_ref.shape[1]
     cap = slot_total // n_space
-    per_group = LANES // cap
+    half_lanes = LANES // 2
+    per_half = half_lanes // cap
+    half_blocks = owned_blocks // 2
 
     me = lax.axis_index("space")
     group = lax.axis_index("mode")
     sibling = group + 1 - 2 * lax.rem(group, 2)
     partner = lax.rem(group + 2, MODE_GROUPS)
-    diagonal = lax.rem(sibling + 2, MODE_GROUPS)
+    half = lax.rem(group, 2)
     others = [lax.rem(me + step, n_space) for step in range(1, n_space)]
 
     barrier = pltpu.get_barrier_semaphore()
@@ -65,10 +67,9 @@
     for other in others:
         pl.semaphore_signal(barrier, inc=1, device_id={"space": other}, device_id_type=MESH)
 
-    chunk_slots = chunk_blocks * stored
+    half_slots = half_blocks * stored
     spans = [pl.ds(owned_blocks * stored, (out_blocks - owned_blocks) * stored)]
-    for step in range(chunk_count):
-        spans.append(pl.ds(lax.rem(group + step, chunk_count) * chunk_slots, chunk_slots))
+    spans += [pl.ds(at * half_slots, half_slots) for at in (half, 1 - half)]
     loads = [
         pltpu.make_async_copy(blocks_hbm.at[:, span], stiff.at[:, span], load_sem.at[at])
         for at, span in enumerate(spans)
@@ -97,11 +98,11 @@
     def field_hop(kind, c):
         return hop(lambda owner: field.at[c, owner], kind, c)
 
-    def sums_hop(kind, p):
-        return hop(lambda owner: sums.at[owner, p], kind, chunk_count + p)
-
-    def arrived_hop(kind):
-        return hop(lambda owner: arrived.at[owner], kind, chunk_count + chunk_blocks)
+    def sums_hop(p):
+        return hop(lambda owner: sums.at[half, p], 0, chunk_count + p)
+
+    def arrived_hop():
+        return hop(lambda owner: arrived.at[half], 0, chunk_count + half_blocks)
 
     for c in range(chunk_count):
         field_hop(1, c).start()
@@ -131,13 +132,18 @@
         return jnp.broadcast_to(row.astype(jnp.float32), (LANES, LANES)).T.astype(jnp.int32)
 
     lanes = lax.broadcasted_iota(jnp.int32, (LANES, LANES), 1)
-    shifted = lanes - lax.rem(me, per_group) * cap
-    position = jnp.where((shifted >= 0) & (shifted < cap), shifted, -slot_total - 1)
-    for at in range(0, send_ref.shape[1], LANES):
-        slots = as_column(send_ref[:, at : at + LANES])
-        for o in range(n_space):
-            hit = position + o * cap == slots
-            pack_map[at : at + LANES, o * LANES : (o + 1) * LANES] = jnp.where(hit, 1.0, 0.0).astype(jnp.bfloat16)
+    interface_rows = send_ref.shape[1]
+    for side in range(2):
+        shifted = lanes - lax.rem(me, per_half) * cap - side * half_lanes
+        position = jnp.where((shifted >= 0) & (shifted < cap), shifted, -slot_total - 1)
+        for at in range(0, interface_rows, LANES):
+            slots = as_column(send_ref[:, at : at + LANES])
+            low = side * interface_rows + at
+            for o in range(n_space):
+                hit = position + o * cap == slots
+                pack_map[low : low + LANES, o * LANES : (o + 1) * LANES] = jnp.where(hit, 1.0, 0.0).astype(
+                    jnp.bfloat16
+                )
     for at in range(0, slot_total, LANES):
         rows = as_column(recv_ref[:, at : at + LANES])
         for b in range(owned_blocks):
@@ -147,18 +153,21 @@
     def row_weights(c):
         return stiff[:, pl.ds(c * stored, stored)].reshape(-1, block_size)
 
-    def own_modes_pair(c):
+    def own_modes(column, k):
+        return mixed[column, k, group]
+
+    def half_modes(column, k):
+        return mixed[column, k, pl.ds(2 * half, 2)].reshape(2 * mode_rows, block_size)
+
+    def pair_product(c, modes):
         picked = [
-            jnp.concatenate(
-                [mixed[cols_ref[s, r], k, group] for k in range(term_count) for s in range(stored)], axis=1
-            )
+            jnp.concatenate([modes(cols_ref[s, r], k) for k in range(term_count) for s in range(stored)], axis=1)
             for r in (c, c + 1)
         ]
         weights = jnp.concatenate([row_weights(c), row_weights(c + 1)], axis=1)
         product = jnp.dot(jnp.concatenate(picked, axis=0), weights, preferred_element_type=jnp.float32)
-        return jnp.concatenate(
-            [product[:mode_rows, :block_size], product[mode_rows:, block_size:]], axis=1
-        )
+        tall = product.shape[0] // 2
+        return jnp.concatenate([product[:tall, :block_size], product[tall:, block_size:]], axis=1)
 
     def all_modes_row(c):
         picked = [
@@ -189,9 +198,14 @@
         )
 
     def send_interface(apply):
-        interface = [own_modes_pair(c).astype(jnp.bfloat16) for c in range(owned_blocks, out_blocks, 2)]
+        modes = half_modes if apply == 0 else own_modes
+        interface = jnp.concatenate(
+            [pair_product(c, modes).astype(jnp.bfloat16) for c in range(owned_blocks, out_blocks, 2)], axis=1
+        )
+        if apply == 0:
+            interface = jnp.concatenate([interface[:mode_rows], interface[mode_rows:]], axis=1)
         packed = jnp.dot(
-            jnp.concatenate(interface, axis=1), pack_map[...], preferred_element_type=jnp.float32
+            interface, pack_map[0 : interface.shape[1], :], preferred_element_type=jnp.float32
         ).astype(jnp.bfloat16)
         for o in range(n_space):
             outbox[apply, o] = packed[:, o * LANES : (o + 1) * LANES]
@@ -203,12 +217,20 @@
         for other in others:
             arrival(apply, other).wait_recv()
         pieces = []
-        for first in range(0, n_space, per_group):
-            piece = inbox[apply, first]
-            for source in range(first + 1, first + per_group):
-                piece = piece + inbox[apply, source]
+        for first in range(0, n_space, per_half):
+            piece = inbox[apply, first].astype(jnp.float32)
+            for source in range(first + 1, first + per_half):
+                piece = piece + inbox[apply, source].astype(jnp.float32)
             pieces.append(piece)
-        return jnp.concatenate(pieces, axis=1)
+        left = lax.broadcasted_iota(jnp.int32, (mode_rows, LANES), 1) < half_lanes
+        low, high = [], []
+        for even, odd in zip(pieces[0::2], pieces[1::2]):
+            low.append(jnp.where(left, even, pltpu.roll(odd, half_lanes, 1)))
+            high.append(jnp.where(left, pltpu.roll(even, half_lanes, 1), odd))
+        low = jnp.concatenate(low, axis=1).astype(jnp.bfloat16)
+        if apply == 1:
+            return low
+        return jnp.concatenate([low, jnp.concatenate(high, axis=1).astype(jnp.bfloat16)], axis=0)
 
     def mix_all(c):
         field_hop(0, c).wait_recv()
@@ -231,39 +253,25 @@
     loads[0].wait()
     send_interface(0)
     loads[1].wait()
-    for p in range(chunk_blocks):
-        sums[group, p] = all_modes_row(group * chunk_blocks + p).astype(jnp.bfloat16)
-        sums_hop(1, p).start()
-        sums_hop(0, p).start()
-    early = chunk_blocks // 2
-    for p in range(early):
-        sums_hop(1, p).wait_recv()
-        sums_hop(2, p).start()
-    arrived[group] = take_interface(0)
-    arrived_hop(1).start()
-    arrived_hop(0).start()
-    for p in range(early, chunk_blocks):
-        sums_hop(1, p).wait_recv()
-        sums_hop(2, p).start()
-    arrived_hop(1).wait_recv()
-    arrived_hop(2).start()
-    arrived_hop(0).wait_recv()
-    arrived_hop(2).wait_recv()
+    for p in range(half_blocks):
+        sums[half, p] = all_modes_row(half * half_blocks + p).astype(jnp.bfloat16)
+        sums_hop(p).start()
+    arrived[half] = take_interface(0)
+    arrived_hop().start()
+    for p in range(half_blocks):
+        sums_hop(p).wait_recv()
+    arrived_hop().wait_recv()
 
     arrived_all = arrived[...].reshape(all_rows, slot_total)
     own_mixer = mixer[:, group].reshape(term_count * mode_rows, LANES)
-    for kind, c in ((None, group), (1, partner), (0, sibling), (2, diagonal)):
-        if kind in (0, 2):
-            for p in range(chunk_blocks):
-                sums_hop(kind, p).wait_recv()
-        at = pl.multiple_of(c * chunk_dofs, chunk_dofs)
-        added = jnp.dot(
-            arrived_all, add_map[:, pl.ds(at, chunk_dofs)], preferred_element_type=jnp.float32
-        )
-        own = jnp.concatenate([sums[c, p] for p in range(chunk_blocks)], axis=1)
+    for c in range(chunk_count):
+        span = slice(c * chunk_dofs, (c + 1) * chunk_dofs)
+        added = jnp.dot(arrived_all, add_map[:, span], preferred_element_type=jnp.float32)
+        blocks_now = range(c * chunk_blocks, (c + 1) * chunk_blocks)
+        own = jnp.concatenate([sums[b // half_blocks, b % half_blocks] for b in blocks_now], axis=1)
         whole = (own.astype(jnp.float32) + added).astype(jnp.bfloat16)
         own_sum[...] = whole.reshape(MODE_GROUPS, mode_rows, chunk_dofs)
-        out_ref[0, :, pl.ds(at, chunk_dofs)] = own_sum[group, 0:modes_dev, :]
+        out_ref[0, :, span] = own_sum[group, 0:modes_dev, :]
         product = jnp.dot(own_mixer, whole, preferred_element_type=jnp.float32).astype(jnp.bfloat16)
         product = product.reshape(term_count, mode_rows, chunk_dofs)
         for b in range(chunk_blocks):
@@ -272,7 +280,7 @@
     send_interface(1)
     for load in loads[2:]:
         load.wait()
-    rows_now = [own_modes_pair(c) for c in range(0, owned_blocks, 2)]
+    rows_now = [pair_product(c, own_modes) for c in range(0, owned_blocks, 2)]
     last_arrived = take_interface(1)
     for c in range(chunk_count):
         span = slice(c * chunk_dofs, (c + 1) * chunk_dofs)
@@ -283,9 +291,9 @@
     for kind in range(3):
         for c in range(chunk_count):
             field_hop(kind, c).wait_send()
-        for p in range(chunk_blocks):
-            sums_hop(kind, p).wait_send()
-        arrived_hop(kind).wait_send()
+    for p in range(half_blocks):
+        sums_hop(p).wait_send()
+    arrived_hop().wait_send()
     for apply in range(2):
         for other in others:
             swap_copy(apply, other).wait_send()
@@ -297,7 +305,6 @@
     mode_rows = -(-modes_dev // 16) * 16
     chunk_count = MODE_GROUPS
     chunk_dofs = owned_dofs // chunk_count
-    chunk_blocks = chunk_dofs // block_size
     owned_blocks = owned_dofs // block_size
     slot_total = recv_row.shape[0]
     interface_rows = send_slot.shape[0]
@@ -319,20 +326,20 @@
         scratch_shapes=[
             pltpu.VMEM(blocks.shape, jnp.bfloat16),
             pltpu.VMEM((chunk_count, MODE_GROUPS, mode_rows, chunk_dofs), jnp.bfloat16),
-            pltpu.VMEM((chunk_count, chunk_blocks, MODE_GROUPS * mode_rows, block_size), jnp.bfloat16),
-            pltpu.VMEM((MODE_GROUPS, mode_rows, slot_total), jnp.bfloat16),
+            pltpu.VMEM((2, owned_blocks // 2, MODE_GROUPS * mode_rows, block_size), jnp.bfloat16),
+            pltpu.VMEM((2, 2 * mode_rows, slot_total), jnp.bfloat16),
             pltpu.VMEM((owned_blocks, term_count, MODE_GROUPS, mode_rows, block_size), jnp.bfloat16),
             pltpu.VMEM((term_count, LANES, LANES), jnp.float32),
             pltpu.VMEM((term_count, MODE_GROUPS, mode_rows, LANES), jnp.float32),
             pltpu.VMEM((term_count, MODE_GROUPS, mode_rows, LANES), jnp.bfloat16),
-            pltpu.VMEM((interface_rows, n_space * LANES), jnp.bfloat16),
+            pltpu.VMEM((2 * interface_rows, n_space * LANES), jnp.bfloat16),
             pltpu.VMEM((slot_total, owned_dofs), jnp.bfloat16),
             pltpu.VMEM((MODE_GROUPS, mode_rows, chunk_dofs), jnp.bfloat16),
             pltpu.VMEM((2, n_space, mode_rows, LANES), jnp.bfloat16),
             pltpu.VMEM((2, n_space, mode_rows, LANES), jnp.bfloat16),
-            pltpu.SemaphoreType.DMA((1 + chunk_count,)),
-            pltpu.SemaphoreType.DMA((3, chunk_count + chunk_blocks + 1)),
-            pltpu.SemaphoreType.DMA((3, chunk_count + chunk_blocks + 1)),
+            pltpu.SemaphoreType.DMA((3,)),
+            pltpu.SemaphoreType.DMA((3, chunk_count + owned_blocks // 2 + 1)),
+            pltpu.SemaphoreType.DMA((3, chunk_count + owned_blocks // 2 + 1)),
             pltpu.SemaphoreType.DMA((2, n_space)),
             pltpu.SemaphoreType.DMA((2, n_space)),
         ],

time: 31.8 us -> 29.5 us (0.928)
  Pallas kernels: 29.4 us -> 27.1 us
    pallas_call x1, Pallas kernels: 29.4 us -> 27.1 us  [local(): call(modes_in, blocks, block_cols.T, send_slot.reshape(1, -1), recv_row.r...]
where the time goes in v5:
time: 29.5 us; the launch traced here: 29.4 us
  Pallas kernels  27.1 us (92%)
  local copies, waits for them, and re-layouts  1.68 us (6%)
  between operations  0.64 us (2%)
    pallas_call x1, Pallas kernels, local(): call(modes_in, blocks, block_cols.T, send_slot.reshape(1, -1), recv_row.r...  27.1 us
    squeeze x1, local copies, waits for them, and re-layouts, local(): return (results[0], results[1])  1.68 us

profile of v5, /device:TPU:0, one launch (start us, length us, event | category | flops | bytes accessed | tf_op | source)
XLA Modules:
  0.0 29.4 jit_solution(11326426830034955549)
XLA Ops:
  0.6 27.1 %shard_map.86 = bf16[2,30,2048]{2,1,0:T(8,128)(2,1)} custom-call(bf16[30,2048]{1,0:T(8,128)(2,1)} %modes_ref.1, bf16[5,72,128,128]{3,2,1,0:T(8,128)(2,1)} %blocks_hbm.1, s32[4,18]{1,0:T(4,128)} %bitcast.11, s32[1,256]{1,0:T(1,128)} %bitcast.13, s32[1,512]{1,0:T(1,128)} %bitcast.12, s32[5,8,120]{2,1,0:T(8,128)} %bitcast.9, f32[5,8,120]{2,1,0:T(8,128)} %bitcast.10), custom_call_target="tpu_custom_call" | custom-call | tf_op jit(solution)/shard_map/pallas_call | solution.py:350
  27.7 1.7 %slice_bitcast_fusion = (bf16[30,2048]{1,0:T(8,128)(2,1)}, bf16[30,2048]{1,0:T(8,128)(2,1)}) fusion(bf16[2,30,2048]{2,1,0:T(8,128)(2,1)} %shard_map.86), kind=kLoop, calls=%fused_computation | loop fusion | bytes 491520 | tf_op jit(solution)/shard_map/squeeze | solution.py:360

commit v6 on v5

--- a/solution.py
+++ b/solution.py
@@ -32,7 +32,7 @@
     mixer,
     pack_map,
     add_map,
-    own_sum,
+    own_mixed,
     outbox,
     inbox,
     load_sem,
@@ -256,28 +256,36 @@
     for p in range(half_blocks):
         sums[half, p] = all_modes_row(half * half_blocks + p).astype(jnp.bfloat16)
         sums_hop(p).start()
-    arrived[half] = take_interface(0)
-    arrived_hop().start()
+    own_mixer = mixer[:, group].reshape(term_count * mode_rows, LANES)
     for p in range(half_blocks):
         sums_hop(p).wait_recv()
-    arrived_hop().wait_recv()
-
-    arrived_all = arrived[...].reshape(all_rows, slot_total)
-    own_mixer = mixer[:, group].reshape(term_count * mode_rows, LANES)
-    for c in range(chunk_count):
-        span = slice(c * chunk_dofs, (c + 1) * chunk_dofs)
-        added = jnp.dot(arrived_all, add_map[:, span], preferred_element_type=jnp.float32)
+    for c in range(chunk_count):
         blocks_now = range(c * chunk_blocks, (c + 1) * chunk_blocks)
         own = jnp.concatenate([sums[b // half_blocks, b % half_blocks] for b in blocks_now], axis=1)
-        whole = (own.astype(jnp.float32) + added).astype(jnp.bfloat16)
-        own_sum[...] = whole.reshape(MODE_GROUPS, mode_rows, chunk_dofs)
-        out_ref[0, :, span] = own_sum[group, 0:modes_dev, :]
-        product = jnp.dot(own_mixer, whole, preferred_element_type=jnp.float32).astype(jnp.bfloat16)
+        own_mixed[c] = jnp.dot(own_mixer, own, preferred_element_type=jnp.float32)
+    arrived[half] = take_interface(0).reshape(2, mode_rows, slot_total)
+    arrived_hop().start()
+    arrived_hop().wait_recv()
+
+    arrived_all = arrived[...].reshape(all_rows, slot_total)
+    arrived_mixed = jnp.dot(own_mixer, arrived_all, preferred_element_type=jnp.float32).astype(jnp.bfloat16)
+    for c in range(chunk_count):
+        span = slice(c * chunk_dofs, (c + 1) * chunk_dofs)
+        added = jnp.dot(arrived_mixed, add_map[:, span], preferred_element_type=jnp.float32)
+        product = (own_mixed[c] + added).astype(jnp.bfloat16)
         product = product.reshape(term_count, mode_rows, chunk_dofs)
         for b in range(chunk_blocks):
             mixed[c * chunk_blocks + b, :, group] = product[:, :, b * block_size : (b + 1) * block_size]
 
     send_interface(1)
+    own_at = pl.ds(pl.multiple_of(group * mode_rows, mode_rows), mode_rows)
+    own_arrived = arrived[group // 2, half]
+    for c in range(chunk_count):
+        span = slice(c * chunk_dofs, (c + 1) * chunk_dofs)
+        added = jnp.dot(own_arrived, add_map[:, span], preferred_element_type=jnp.float32)
+        blocks_now = range(c * chunk_blocks, (c + 1) * chunk_blocks)
+        own = jnp.concatenate([sums[b // half_blocks, b % half_blocks, own_at, :] for b in blocks_now], axis=1)
+        out_ref[0, :, span] = (own.astype(jnp.float32) + added)[0:modes_dev, :].astype(jnp.bfloat16)
     for load in loads[2:]:
         load.wait()
     rows_now = [pair_product(c, own_modes) for c in range(0, owned_blocks, 2)]
@@ -327,14 +335,14 @@
             pltpu.VMEM(blocks.shape, jnp.bfloat16),
             pltpu.VMEM((chunk_count, MODE_GROUPS, mode_rows, chunk_dofs), jnp.bfloat16),
             pltpu.VMEM((2, owned_blocks // 2, MODE_GROUPS * mode_rows, block_size), jnp.bfloat16),
-            pltpu.VMEM((2, 2 * mode_rows, slot_total), jnp.bfloat16),
+            pltpu.VMEM((2, 2, mode_rows, slot_total), jnp.bfloat16),
             pltpu.VMEM((owned_blocks, term_count, MODE_GROUPS, mode_rows, block_size), jnp.bfloat16),
             pltpu.VMEM((term_count, LANES, LANES), jnp.float32),
             pltpu.VMEM((term_count, MODE_GROUPS, mode_rows, LANES), jnp.float32),
             pltpu.VMEM((term_count, MODE_GROUPS, mode_rows, LANES), jnp.bfloat16),
             pltpu.VMEM((2 * interface_rows, n_space * LANES), jnp.bfloat16),
             pltpu.VMEM((slot_total, owned_dofs), jnp.bfloat16),
-            pltpu.VMEM((MODE_GROUPS, mode_rows, chunk_dofs), jnp.bfloat16),
+            pltpu.VMEM((chunk_count, term_count * mode_rows, chunk_dofs), jnp.float32),
             pltpu.VMEM((2, n_space, mode_rows, LANES), jnp.bfloat16),
             pltpu.VMEM((2, n_space, mode_rows, LANES), jnp.bfloat16),
             pltpu.SemaphoreType.DMA((3,)),

time: 29.5 us -> 28.9 us (0.980)
  Pallas kernels: 27.1 us -> 26.5 us
    pallas_call x1, Pallas kernels: 27.1 us -> 26.5 us  [local(): call(modes_in, blocks, block_cols.T, send_slot.reshape(1, -1), recv_row.r...]
where the time goes in v6:
time: 28.9 us; the launch traced here: 28.8 us
  Pallas kernels  26.5 us (92%)
  local copies, waits for them, and re-layouts  1.68 us (6%)
  between operations  0.64 us (2%)
    pallas_call x1, Pallas kernels, local(): call(modes_in, blocks, block_cols.T, send_slot.reshape(1, -1), recv_row.r...  26.5 us
    squeeze x1, local copies, waits for them, and re-layouts, local(): return (results[0], results[1])  1.68 us

profile of v6, /device:TPU:0, one launch (start us, length us, event | category | flops | bytes accessed | tf_op | source)
XLA Modules:
  0.0 28.8 jit_solution(11800946959785799278)
XLA Ops:
  0.6 26.5 %shard_map.86 = bf16[2,30,2048]{2,1,0:T(8,128)(2,1)} custom-call(bf16[30,2048]{1,0:T(8,128)(2,1)} %modes_ref.1, bf16[5,72,128,128]{3,2,1,0:T(8,128)(2,1)} %blocks_hbm.1, s32[4,18]{1,0:T(4,128)} %bitcast.11, s32[1,256]{1,0:T(1,128)} %bitcast.13, s32[1,512]{1,0:T(1,128)} %bitcast.12, s32[5,8,120]{2,1,0:T(8,128)} %bitcast.9, f32[5,8,120]{2,1,0:T(8,128)} %bitcast.10), custom_call_target="tpu_custom_call" | custom-call | tf_op jit(solution)/shard_map/pallas_call | solution.py:358
  27.1 1.7 %slice_bitcast_fusion = (bf16[30,2048]{1,0:T(8,128)(2,1)}, bf16[30,2048]{1,0:T(8,128)(2,1)}) fusion(bf16[2,30,2048]{2,1,0:T(8,128)(2,1)} %shard_map.86), kind=kLoop, calls=%fused_computation | loop fusion | bytes 491520 | tf_op jit(solution)/shard_map/squeeze | solution.py:368

commit v7 on v6

--- a/solution.py
+++ b/solution.py
@@ -133,22 +133,28 @@
 
     lanes = lax.broadcasted_iota(jnp.int32, (LANES, LANES), 1)
     interface_rows = send_ref.shape[1]
-    for side in range(2):
-        shifted = lanes - lax.rem(me, per_half) * cap - side * half_lanes
-        position = jnp.where((shifted >= 0) & (shifted < cap), shifted, -slot_total - 1)
-        for at in range(0, interface_rows, LANES):
-            slots = as_column(send_ref[:, at : at + LANES])
-            low = side * interface_rows + at
-            for o in range(n_space):
-                hit = position + o * cap == slots
-                pack_map[low : low + LANES, o * LANES : (o + 1) * LANES] = jnp.where(hit, 1.0, 0.0).astype(
+
+    def fill_pack_map():
+        for side in range(2):
+            shifted = lanes - lax.rem(me, per_half) * cap - side * half_lanes
+            position = jnp.where((shifted >= 0) & (shifted < cap), shifted, -slot_total - 1)
+            for at in range(0, interface_rows, LANES):
+                slots = as_column(send_ref[:, at : at + LANES])
+                low = side * interface_rows + at
+                for o in range(n_space):
+                    hit = position + o * cap == slots
+                    pack_map[low : low + LANES, o * LANES : (o + 1) * LANES] = jnp.where(hit, 1.0, 0.0).astype(
+                        jnp.bfloat16
+                    )
+
+    def fill_add_map(first, last):
+        for at in range(first, last, LANES):
+            rows = as_column(recv_ref[:, at : at + LANES])
+            for b in range(owned_blocks):
+                hit = lanes + b * LANES == rows
+                add_map[at : at + LANES, b * LANES : (b + 1) * LANES] = jnp.where(hit, 1.0, 0.0).astype(
                     jnp.bfloat16
                 )
-    for at in range(0, slot_total, LANES):
-        rows = as_column(recv_ref[:, at : at + LANES])
-        for b in range(owned_blocks):
-            hit = lanes + b * LANES == rows
-            add_map[at : at + LANES, b * LANES : (b + 1) * LANES] = jnp.where(hit, 1.0, 0.0).astype(jnp.bfloat16)
 
     def row_weights(c):
         return stiff[:, pl.ds(c * stored, stored)].reshape(-1, block_size)
@@ -232,26 +238,35 @@
             return low
         return jnp.concatenate([low, jnp.concatenate(high, axis=1).astype(jnp.bfloat16)], axis=0)
 
-    def mix_all(c):
+    def mix_groups(c, groups):
+        whole = field[c].reshape(all_rows, chunk_dofs)
+        product = jnp.dot(
+            mixer[:, groups].reshape(-1, LANES), whole, preferred_element_type=jnp.float32
+        ).astype(jnp.bfloat16)
+        product = product.reshape(term_count, -1, mode_rows, chunk_dofs)
+        for b in range(chunk_blocks):
+            mixed[c * chunk_blocks + b, :, groups] = product[..., b * block_size : (b + 1) * block_size]
+
+    def take_field(c):
         field_hop(0, c).wait_recv()
         field_hop(2, c).wait_recv()
-        whole = field[c].reshape(all_rows, chunk_dofs)
-        product = jnp.dot(
-            mixer[...].reshape(term_count * all_rows, LANES), whole, preferred_element_type=jnp.float32
-        ).astype(jnp.bfloat16)
-        product = product.reshape(term_count, MODE_GROUPS, mode_rows, chunk_dofs)
-        for b in range(chunk_blocks):
-            mixed[c * chunk_blocks + b] = product[..., b * block_size : (b + 1) * block_size]
 
     for c in range(chunk_count):
         field_hop(1, c).wait_recv()
         field_hop(2, c).start()
+        if c == 0:
+            fill_pack_map()
+        elif c < chunk_count - 1:
+            middle = slot_total // 2
+            fill_add_map(*((0, middle) if c == 1 else (middle, slot_total)))
         if c > 0:
-            mix_all(c - 1)
-    mix_all(chunk_count - 1)
-
+            take_field(c - 1)
+            mix_groups(c - 1, slice(None))
+    take_field(chunk_count - 1)
+    mix_groups(chunk_count - 1, pl.ds(2 * half, 2))
     loads[0].wait()
     send_interface(0)
+    mix_groups(chunk_count - 1, pl.ds(2 - 2 * half, 2))
     loads[1].wait()
     for p in range(half_blocks):
         sums[half, p] = all_modes_row(half * half_blocks + p).astype(jnp.bfloat16)

time: 28.9 us -> 29.1 us (level)
  no operation moved by 1% of the time
where the time goes in v7:
time: 29.1 us; the launch traced here: 29 us
  Pallas kernels  26.6 us (91%)
  local copies, waits for them, and re-layouts  1.68 us (6%)
  between operations  0.64 us (2%)
    pallas_call x1, Pallas kernels, local(): call(modes_in, blocks, block_cols.T, send_slot.reshape(1, -1), recv_row.r...  26.6 us
    squeeze x1, local copies, waits for them, and re-layouts, local(): return (results[0], results[1])  1.68 us

profile of v7, /device:TPU:0, one launch (start us, length us, event | category | flops | bytes accessed | tf_op | source)
XLA Modules:
  0.0 29.0 jit_solution(11374331626839159589)
XLA Ops:
  0.6 26.6 %shard_map.86 = bf16[2,30,2048]{2,1,0:T(8,128)(2,1)} custom-call(bf16[30,2048]{1,0:T(8,128)(2,1)} %modes_ref.1, bf16[5,72,128,128]{3,2,1,0:T(8,128)(2,1)} %blocks_hbm.1, s32[4,18]{1,0:T(4,128)} %bitcast.11, s32[1,256]{1,0:T(1,128)} %bitcast.13, s32[1,512]{1,0:T(1,128)} %bitcast.12, s32[5,8,120]{2,1,0:T(8,128)} %bitcast.9, f32[5,8,120]{2,1,0:T(8,128)} %bitcast.10), custom_call_target="tpu_custom_call" | custom-call | tf_op jit(solution)/shard_map/pallas_call | solution.py:373
  27.3 1.7 %slice_bitcast_fusion = (bf16[30,2048]{1,0:T(8,128)(2,1)}, bf16[30,2048]{1,0:T(8,128)(2,1)}) fusion(bf16[2,30,2048]{2,1,0:T(8,128)(2,1)} %shard_map.86), kind=kLoop, calls=%fused_computation | loop fusion | bytes 491520 | tf_op jit(solution)/shard_map/squeeze | solution.py:383
